TPU v7x, 32 devices: a whole 2x2x4 slice. The times are simulated.
32 devices in a mesh: dp: 8 (over y, x, core), seq: 4 (over z).
Axes of the slice: x: 2, y: 2, z: 4, core: 2. Of those that a mesh axis runs over, the one named last changes fastest.
Arguments:
- hidden: bfloat16 [32, 272, 1152], P(('dp', 'seq')), may hold values from -6 to 6
- skipped: bfloat16 [32, 272, 1152], P(('dp', 'seq')), may hold values from -6 to 6
- row_mask: int32 [32, 272], P('dp'), may hold values from 0 to 1, as said below
- cotangent: bfloat16 [32, 272, 1152], P(('dp', 'seq')), may hold values from -6 to 6
- merge_weight: bfloat16 [2304, 1152], P('seq'), may hold values from -0.125 to 0.125
- merge_bias: bfloat16 [1152], replicated, may hold values from -1.75 to 1.75
- first_gain: bfloat16 [1152], replicated, may hold values from 0.099609375 to 1.8984375
- first_shift: bfloat16 [1152], replicated, may hold values from -1.75 to 1.75
- triple_weight: bfloat16 [1152, 3456], P('seq'), may hold values from -0.1875 to 0.1875
- output_weight: bfloat16 [1152, 1152], P('seq'), may hold values from -1 to 1
- output_bias: bfloat16 [1152], replicated, may hold values from -1.75 to 1.75
- second_gain: bfloat16 [1152], replicated, may hold values from 0.099609375 to 1.8984375
- second_shift: bfloat16 [1152], replicated, may hold values from -1.75 to 1.75
- expand_weight: bfloat16 [1152, 4608], P('seq'), may hold values from -0.1875 to 0.1875
- expand_bias: bfloat16 [4608], replicated, may hold values from -1.75 to 1.75
- reduce_weight: bfloat16 [4608, 1152], P('seq'), may hold values from -0.09375 to 0.09375
- reduce_bias: bfloat16 [1152], replicated, may hold values from -1.75 to 1.75
Outputs:
- result: bfloat16 [32, 272, 1152], P(('dp', 'seq'))
- hidden_grad: bfloat16 [32, 272, 1152], P(('dp', 'seq'))
- skipped_grad: bfloat16 [32, 272, 1152], P(('dp', 'seq'))
- merge_weight_grad: float32 [2304, 1152], P('seq')
- merge_bias_grad: float32 [1152], replicated
- first_gain_grad: float32 [1152], replicated
- first_shift_grad: float32 [1152], replicated
- triple_weight_grad: float32 [1152, 3456], P('seq')
- output_weight_grad: float32 [1152, 1152], P('seq')
- output_bias_grad: float32 [1152], replicated
- second_gain_grad: float32 [1152], replicated
- second_shift_grad: float32 [1152], replicated
- expand_weight_grad: float32 [1152, 4608], P('seq')
- expand_bias_grad: float32 [4608], replicated
- reduce_weight_grad: float32 [4608, 1152], P('seq')
- reduce_bias_grad: float32 [1152], replicated
Inputs may be any that keep to these rules, and one draw needn't show every extreme that they name: `row_mask`: in each image exactly 258 of the 272 rows are 1; which ones is drawn from the seed.
All inputs are finite; a program needn't handle non-finite values.
Results may differ from a plain program's by a relative error of at most 0.02.
Values may be sent and summed in bfloat16 or wider, within the bound.
A program may use at most 256 MiB of HBM per device.

v0:
```python
from functools import partial

import jax
import jax.numpy as jnp
from jax import lax
from jax.sharding import PartitionSpec as P

HEADS = 16


EPS = 1e-05
NEGATIVE = -1e30


def layer_norm(values, gain, shift):
    center = jnp.mean(values, axis=-1, keepdims=True)
    centred = values - center
    spread = jnp.mean(centred * centred, axis=-1, keepdims=True)
    return centred * lax.rsqrt(spread + EPS) * gain + shift


def against(left, right):
    return lax.dot_general(
        left, right, (((1,), (1,)), ((), ())), preferred_element_type=jnp.float32
    )


def weight_grad(left, right):
    return lax.dot_general(
        left, right, (((0,), (0,)), ((), ())), preferred_element_type=jnp.float32
    )


def masked_scores(queries, key_heads, valid):
    scaling = queries.shape[-1] ** (-0.5)
    scores = (
        jnp.einsum("bqhd,bkhd->bhqk", queries, key_heads, preferred_element_type=jnp.float32)
        * scaling
    )
    return jnp.where(valid[:, None, None, :] > 0, scores, NEGATIVE)


def attention_block(inputs):
    queries, key_heads, value_heads, valid = inputs
    scores = masked_scores(queries, key_heads, valid)
    row_peak = jnp.max(scores, axis=-1, keepdims=True)
    log_total = row_peak + jnp.log(jnp.sum(jnp.exp(scores - row_peak), axis=-1, keepdims=True))
    attention = jnp.exp(scores - log_total).astype(jnp.bfloat16)
    attended = jnp.einsum(
        "bhqk,bkhd->bqhd", attention, value_heads, preferred_element_type=jnp.float32
    )
    return (attended.astype(jnp.bfloat16), log_total)


def attention_back(inputs):
    queries, key_heads, value_heads, valid, log_total, upstream = inputs
    scaling = queries.shape[-1] ** (-0.5)
    scores = masked_scores(queries, key_heads, valid)
    attention = jnp.exp(scores - log_total)
    prob_grad = jnp.einsum(
        "bqhd,bkhd->bhqk", upstream, value_heads, preferred_element_type=jnp.float32
    )
    values_grad = jnp.einsum(
        "bhqk,bqhd->bkhd",
        attention.astype(jnp.bfloat16),
        upstream,
        preferred_element_type=jnp.float32,
    )
    row_delta = jnp.sum(attention * prob_grad, axis=-1, keepdims=True)
    score_grad = (attention * (prob_grad - row_delta)).astype(jnp.bfloat16)
    queries_grad = (
        jnp.einsum("bhqk,bkhd->bqhd", score_grad, key_heads, preferred_element_type=jnp.float32)
        * scaling
    )
    keys_grad = (
        jnp.einsum("bhqk,bqhd->bkhd", score_grad, queries, preferred_element_type=jnp.float32)
        * scaling
    )
    return (
        queries_grad.astype(jnp.bfloat16),
        keys_grad.astype(jnp.bfloat16),
        values_grad.astype(jnp.bfloat16),
    )


def body(
    hidden,
    skipped,
    row_mask,
    cotangent,
    merge_weight,
    merge_bias,
    first_gain,
    first_shift,
    triple_weight,
    output_weight,
    output_bias,
    second_gain,
    second_shift,
    expand_weight,
    expand_bias,
    reduce_weight,
    reduce_bias,
):
    images, length, model_width = hidden.shape
    row_count = images * length
    seq_count = lax.axis_size("seq")
    heads_here = HEADS // seq_count
    head_size = model_width // HEADS
    group_images = images * seq_count
    merge_full, triple_full, output_full, expand_full, reduce_full = (
        lax.all_gather(merge_weight, "seq", axis=0, tiled=True),
        lax.all_gather(triple_weight, "seq", axis=0, tiled=True),
        lax.all_gather(output_weight, "seq", axis=0, tiled=True),
        lax.all_gather(expand_weight, "seq", axis=0, tiled=True),
        lax.all_gather(reduce_weight, "seq", axis=0, tiled=True),
    )
    gain_a = first_gain.astype(jnp.float32)
    shift_a = first_shift.astype(jnp.float32)
    gain_b = second_gain.astype(jnp.float32)
    shift_b = second_shift.astype(jnp.float32)
    joined = jnp.concatenate([hidden, skipped], axis=-1).reshape(row_count, 2 * model_width)
    merged = jnp.dot(joined, merge_full, preferred_element_type=jnp.float32) + merge_bias.astype(
        jnp.float32
    )
    normed = layer_norm(merged, gain_a, shift_a).astype(jnp.bfloat16)
    triple = jnp.dot(normed, triple_full, preferred_element_type=jnp.float32).astype(jnp.bfloat16)
    triple = triple.reshape(images, length, 3 * model_width)
    query_rows = triple[..., :model_width]
    key_rows = triple[..., model_width : 2 * model_width]
    value_rows = triple[..., 2 * model_width :]
    queries, key_heads, value_heads = (
        lax.all_to_all(query_rows, "seq", split_axis=2, concat_axis=0, tiled=True),
        lax.all_to_all(key_rows, "seq", split_axis=2, concat_axis=0, tiled=True),
        lax.all_to_all(value_rows, "seq", split_axis=2, concat_axis=0, tiled=True),
    )
    per_block = 1
    while per_block < group_images and (per_block * length < 512 or group_images % per_block != 0):
        per_block += 1
    blocks = group_images // per_block

    def split_blocks(array):
        return array.reshape((blocks, per_block) + array.shape[1:])

    def split_heads(array):
        return split_blocks(array.reshape(group_images, length, heads_here, head_size))

    query_blocks = split_heads(queries)
    key_blocks = split_heads(key_heads)
    value_blocks = split_heads(value_heads)
    mask_blocks = split_blocks(row_mask)
    attended_heads, log_totals = lax.map(
        attention_block, (query_blocks, key_blocks, value_blocks, mask_blocks)
    )
    attended_heads = attended_heads.reshape(group_images, length, heads_here * head_size)
    attended = lax.all_to_all(
        attended_heads, "seq", split_axis=0, concat_axis=2, tiled=True
    ).reshape(row_count, model_width)
    middle = (
        merged
        + jnp.dot(attended, output_full, preferred_element_type=jnp.float32)
        + output_bias.astype(jnp.float32)
    )
    normed_two = layer_norm(middle, gain_b, shift_b).astype(jnp.bfloat16)
    expanded = jnp.dot(
        normed_two, expand_full, preferred_element_type=jnp.float32
    ) + expand_bias.astype(jnp.float32)
    activated = jax.nn.gelu(expanded, approximate=False).astype(jnp.bfloat16)
    result = (
        middle
        + jnp.dot(activated, reduce_full, preferred_element_type=jnp.float32)
        + reduce_bias.astype(jnp.float32)
    )
    result = result.astype(jnp.bfloat16).reshape(images, length, model_width)
    upstream = cotangent.reshape(row_count, model_width)
    upstream_wide = upstream.astype(jnp.float32)
    reduce_grad = weight_grad(activated, upstream)
    reduce_bias_part = jnp.sum(upstream_wide, axis=0)
    activated_grad = against(upstream, reduce_full)
    ignored, gelu_back = jax.vjp(partial(jax.nn.gelu, approximate=False), expanded)
    expanded_grad = gelu_back(activated_grad)[0].astype(jnp.bfloat16)
    expand_grad = weight_grad(normed_two, expanded_grad)
    expand_bias_part = jnp.sum(expanded_grad.astype(jnp.float32), axis=0)
    ignored, second_back = jax.vjp(layer_norm, middle, gain_b, shift_b)
    middle_norm_grad, gain_b_part, shift_b_part = second_back(against(expanded_grad, expand_full))
    middle_grad = upstream_wide + middle_norm_grad
    branch_grad = middle_grad.astype(jnp.bfloat16)
    output_grad = weight_grad(attended, branch_grad)
    output_bias_part = jnp.sum(branch_grad.astype(jnp.float32), axis=0)
    attended_grad = (
        against(branch_grad, output_full).astype(jnp.bfloat16).reshape(images, length, model_width)
    )
    heads_grad = lax.all_to_all(attended_grad, "seq", split_axis=2, concat_axis=0, tiled=True)
    queries_grad, keys_grad, values_grad = lax.map(
        attention_back,
        (query_blocks, key_blocks, value_blocks, mask_blocks, log_totals, split_heads(heads_grad)),
    )
    queries_grad = queries_grad.reshape(group_images, length, heads_here * head_size)
    keys_grad = keys_grad.reshape(group_images, length, heads_here * head_size)
    values_grad = values_grad.reshape(group_images, length, heads_here * head_size)
    query_rows_grad, key_rows_grad, value_rows_grad = (
        lax.all_to_all(queries_grad, "seq", split_axis=0, concat_axis=2, tiled=True),
        lax.all_to_all(keys_grad, "seq", split_axis=0, concat_axis=2, tiled=True),
        lax.all_to_all(values_grad, "seq", split_axis=0, concat_axis=2, tiled=True),
    )
    triple_grad = jnp.concatenate(
        [query_rows_grad, key_rows_grad, value_rows_grad], axis=-1
    ).reshape(row_count, 3 * model_width)
    triple_part = weight_grad(normed, triple_grad)
    ignored, first_back = jax.vjp(layer_norm, merged, gain_a, shift_a)
    merged_norm_grad, gain_a_part, shift_a_part = first_back(against(triple_grad, triple_full))
    merged_grad = (middle_grad + merged_norm_grad).astype(jnp.bfloat16)
    merge_grad = weight_grad(joined, merged_grad)
    merge_bias_part = jnp.sum(merged_grad.astype(jnp.float32), axis=0)
    joined_grad = against(merged_grad, merge_full)
    hidden_grad = (
        joined_grad[:, :model_width].astype(jnp.bfloat16).reshape(images, length, model_width)
    )
    skipped_grad = (
        joined_grad[:, model_width:].astype(jnp.bfloat16).reshape(images, length, model_width)
    )
    merge_rows, triple_rows, output_rows, expand_rows, reduce_rows = (
        lax.psum_scatter(
            merge_grad.astype(jnp.bfloat16), "seq", scatter_dimension=0, tiled=True
        ).astype(jnp.float32),
        lax.psum_scatter(
            triple_part.astype(jnp.bfloat16), "seq", scatter_dimension=0, tiled=True
        ).astype(jnp.float32),
        lax.psum_scatter(
            output_grad.astype(jnp.bfloat16), "seq", scatter_dimension=0, tiled=True
        ).astype(jnp.float32),
        lax.psum_scatter(
            expand_grad.astype(jnp.bfloat16), "seq", scatter_dimension=0, tiled=True
        ).astype(jnp.float32),
        lax.psum_scatter(
            reduce_grad.astype(jnp.bfloat16), "seq", scatter_dimension=0, tiled=True
        ).astype(jnp.float32),
    )
    merge_sum, triple_sum, output_sum, expand_sum, reduce_sum = (
        lax.psum(merge_rows.astype(jnp.bfloat16), "dp").astype(jnp.float32),
        lax.psum(triple_rows.astype(jnp.bfloat16), "dp").astype(jnp.float32),
        lax.psum(output_rows.astype(jnp.bfloat16), "dp").astype(jnp.float32),
        lax.psum(expand_rows.astype(jnp.bfloat16), "dp").astype(jnp.float32),
        lax.psum(reduce_rows.astype(jnp.bfloat16), "dp").astype(jnp.float32),
    )
    (
        merge_bias_sum,
        gain_a_sum,
        shift_a_sum,
        output_bias_sum,
        gain_b_sum,
        shift_b_sum,
        expand_bias_sum,
        reduce_bias_sum,
    ) = lax.psum(
        (
            merge_bias_part,
            gain_a_part,
            shift_a_part,
            output_bias_part,
            gain_b_part,
            shift_b_part,
            expand_bias_part,
            reduce_bias_part,
        ),
        ("dp", "seq"),
    )
    return (
        result,
        hidden_grad,
        skipped_grad,
        merge_sum,
        merge_bias_sum,
        gain_a_sum,
        shift_a_sum,
        triple_sum,
        output_sum,
        output_bias_sum,
        gain_b_sum,
        shift_b_sum,
        expand_sum,
        expand_bias_sum,
        reduce_sum,
        reduce_bias_sum,
    )


def solution(mesh):
    return jax.shard_map(
        body,
        mesh=mesh,
        in_specs=(
            P(("dp", "seq"), None, None),
            P(("dp", "seq"), None, None),
            P("dp", None),
            P(("dp", "seq"), None, None),
            P("seq", None),
            P(),
            P(),
            P(),
            P("seq", None),
            P("seq", None),
            P(),
            P(),
            P(),
            P("seq", None),
            P(),
            P("seq", None),
            P(),
        ),
        out_specs=(
            P(("dp", "seq"), None, None),
            P(("dp", "seq"), None, None),
            P(("dp", "seq"), None, None),
            P("seq", None),
            P(),
            P(),
            P(),
            P("seq", None),
            P("seq", None),
            P(),
            P(),
            P(),
            P("seq", None),
            P(),
            P("seq", None),
            P(),
        ),
        check_vma=False,
    )
```

profile of v0, /device:TPU:0, one launch (start us, length us, event | category | flops | bytes accessed | tf_op | source)
XLA Modules:
  0.0 1682.2 jit_solution(8403484208499835470)
XLA Ops:
  10.7 100.8 %all-gather.6.cloned.1.call-done = bf16[2304,1152]{1,0:T(8,128)(2,1)} async-done(((bf16[576,1152]{1,0:T(8,128)(2,1)}), bf16[2304,1152]{1,0:T(8,128)(2,1)}) %all-gather.6.cloned.1.call-update) | async-done | bytes 5308432 | tf_op jit(solution)/shard_map/all_gather | solution.py:112
  116.9 137.2 %all-gather.8.cloned.1.call-done = bf16[1152,3456]{1,0:T(8,128)(2,1)} async-done(((bf16[288,3456]{1,0:T(8,128)(2,1)}), bf16[1152,3456]{1,0:T(8,128)(2,1)}) %all-gather.8.cloned.1.call-update) | async-done | bytes 7962640 | tf_op jit(solution)/shard_map/all_gather | solution.py:113
  254.1 6.0 fusion.63
  265.7 6.3 reduce.2
  282.8 6.3 reduce.1
  291.2 20.7 %all-to-all-done.2 = bf16[4,2,39168]{2,1,0:T(2,128)(2,1)} async-done(((bf16[4,2,39168]{2,1,0:T(2,128)(2,1)}), bf16[4,2,39168]{2,1,0:T(2,128)(2,1)}, u32[]{:S(2)}, u32[]{:S(2)}) %all-to-all-start.2) | async-done | bytes 626720 | tf_op jit(solution)/shard_map/all_to_all | solution.py:134
  320.6 6.3 reduce
  329.0 6.6 all-to-all-done.1
  358.2 19.6 %all-to-all-done = bf16[4,2,39168]{2,1,0:T(2,128)(2,1)} async-done(((bf16[4,2,39168]{2,1,0:T(2,128)(2,1)}), bf16[4,2,39168]{2,1,0:T(2,128)(2,1)}, u32[]{:S(2)}, u32[]{:S(2)}) %all-to-all-start) | async-done | bytes 626720 | tf_op jit(solution)/shard_map/all_to_all | solution.py:135
  402.0 35.8 %all-to-all-done.3 = bf16[4,272,288]{2,1,0:T(8,128)(2,1)S(1)} async-done(((bf16[4,272,288]{2,1,0:T(8,128)(2,1)}), bf16[4,272,288]{2,1,0:T(8,128)(2,1)S(1)}, u32[]{:S(2)}, u32[]{:S(2)}) %all-to-all-start.3) | async-done | bytes 626720 | tf_op jit(solution)/shard_map/all_to_all | solution.py:156
  445.8 100.2 %all-gather.12.cloned.1.call-done = bf16[1152,4608]{1,0:T(8,128)(2,1)} async-done(((bf16[288,4608]{1,0:T(8,128)(2,1)}), bf16[1152,4608]{1,0:T(8,128)(2,1)}) %all-gather.12.cloned.1.call-update) | async-done | bytes 10616848 | tf_op jit(solution)/shard_map/all_gather | solution.py:115
  546.0 18.6 %multiply_convert_fusion.1 = (bf16[272,4608]{1,0:T(8,128)(2,1)}, f32[272,4608]{1,0:T(8,128)}, f32[272,4608]{1,0:T(8,128)}) fusion(f32[4608]{0:T(1024)S(1)} %convert_element_type.147, bf16[1152,4608]{1,0:T(8,128)(2,1)} %all-gather.12.cloned.1.call-done, f32[272,1152]{1,0:T(8,128)} %copy-done.4, f32[1152]{0:T(1024)S(1)} %convert_element_type.145, ...), kind=kOutput, calls=%fused_computation.75 | convolution fusion | flops 2972067840 | bytes 24433792 | tf_op jit(solution)/shard_map/dot_general | solution.py:165
  564.6 168.1 %all-gather.14.cloned.1.call-done = bf16[4608,1152]{1,0:T(8,128)(2,1)} async-done(((bf16[1152,1152]{1,0:T(8,128)(2,1)}), bf16[4608,1152]{1,0:T(8,128)(2,1)}) %all-gather.14.cloned.1.call-update) | async-done | bytes 10616848 | tf_op jit(solution)/shard_map/all_gather | solution.py:116
  732.7 15.6 convert_reduce_fusion
  748.3 9.0 multiply_reduce_fusion.1
  765.1 7.4 reduce.3
  782.6 21.0 %all-to-all-done.4 = bf16[4,2,39168]{2,1,0:T(2,128)(2,1)S(1)} async-done(((bf16[4,2,39168]{2,1,0:T(2,128)(2,1)}), bf16[4,2,39168]{2,1,0:T(2,128)(2,1)S(1)}, u32[]{:S(2)}, u32[]{:S(2)}) %all-to-all-start.4) | async-done | bytes 626720 | tf_op jit(solution)/shard_map/all_to_all | solution.py:193
  818.4 15.7 while.27
  841.3 14.4 all-to-all-done.5
  860.6 16.9 %all-to-all-done.7 = bf16[4,272,288]{2,1,0:T(8,128)(2,1)S(1)} async-done(((bf16[4,272,288]{2,1,0:T(8,128)(2,1)}), bf16[4,272,288]{2,1,0:T(8,128)(2,1)S(1)}, u32[]{:S(2)}, u32[]{:S(2)}) %all-to-all-start.7) | async-done | bytes 626720 | tf_op jit(solution)/shard_map/all_to_all | solution.py:204
  884.5 16.1 all-to-all-done.6
  901.5 6.7 multiply_reduce_fusion.2
  916.5 7.9 convolution_convert_fusion.2
  925.8 10.0 convolution_convert_fusion.1
  935.8 10.8 convolution_convert_fusion
  946.7 62.8 %reduce-scatter.6.cloned.1.call-done = bf16[576,1152]{1,0:T(8,128)(2,1)} async-done(((bf16[2304,1152]{1,0:T(8,128)(2,1)}), bf16[576,1152]{1,0:T(8,128)(2,1)}) %reduce-scatter.6.cloned.1.call-update) | async-done | bytes 1327120 | tf_op jit(solution)/shard_map/reduce_scatter | solution.py:223
  1009.5 141.1 %reduce-scatter.8.cloned.1.call-done = bf16[288,3456]{1,0:T(8,128)(2,1)} async-done(((bf16[1152,3456]{1,0:T(8,128)(2,1)}), bf16[288,3456]{1,0:T(8,128)(2,1)}) %reduce-scatter.8.cloned.1.call-update) | async-done | bytes 1990672 | tf_op jit(solution)/shard_map/reduce_scatter | solution.py:226
  1150.6 183.1 %reduce-scatter.12.cloned.1.call-done = bf16[288,4608]{1,0:T(8,128)(2,1)} async-done(((bf16[1152,4608]{1,0:T(8,128)(2,1)}), bf16[288,4608]{1,0:T(8,128)(2,1)}) %reduce-scatter.12.cloned.1.call-update) | async-done | bytes 2654224 | tf_op jit(solution)/shard_map/reduce_scatter | solution.py:232
  1333.7 183.5 %reduce-scatter.14.cloned.1.call-done = bf16[1152,1152]{1,0:T(8,128)(2,1)} async-done(((bf16[4608,1152]{1,0:T(8,128)(2,1)}), bf16[1152,1152]{1,0:T(8,128)(2,1)}) %reduce-scatter.14.cloned.1.call-update) | async-done | bytes 2654224 | tf_op jit(solution)/shard_map/reduce_scatter | solution.py:235
  1518.0 9.0 fusion.68
  1527.0 45.1 %all-reduce = (f32[1152]{0:T(1024)}, f32[1152]{0:T(1024)}, f32[1152]{0:T(1024)}, f32[1152]{0:T(1024)}, f32[1152]{0:T(1024)}, /*index=5*/f32[1152]{0:T(1024)}, f32[4608]{0:T(1024)}, f32[1152]{0:T(1024)}) all-reduce(f32[1152]{0:T(1024)S(1)} %get-tuple-element.187, ...), channel_id=1, replica_groups=mesh['dp'=8,'seq'=4] {'dp','seq'}, use_global_device_ids=true, to_apply=%region_18.19 | all-reduce | flops 12672 | bytes 101376 | tf_op jit(solution)/shard_map/psum | solution.py:255
  1577.6 84.5 %all-reduce.4.cloned.1.call-done = (bf16[576,1152]{1,0:T(8,128)(2,1)}, bf16[288,3456]{1,0:T(8,128)(2,1)}, bf16[288,1152]{1,0:T(8,128)(2,1)}, bf16[288,4608]{1,0:T(8,128)(2,1)}, bf16[1152,1152]{1,0:T(8,128)(2,1)}) async-done(((bf16[576,1152]{1,0:T(8,128)(2,1)}, bf16[288,3456]{1,0:T(8,128)(2,1)}, bf16[288,1152]{1,0:T(8,128)(2,1)}, bf16[288,4608]{1,0:T(8,128)(2,1)}, bf16[1152,1152]{1,0:T(8,128)(2,1)}), ...) | async-done | bytes 9289744 | tf_op jit(solution)/shard_map/psum | solution.py:240
  (275 shorter events, 195.0 us)
Async XLA Ops:
  7.2 104.3 %all-gather.6.cloned.1.call-start = ((), (), s32[]{:S(2)}) async-start(), calls=%async_computation.13 | async-start | bytes 6635520 | tf_op jit(solution)/shard_map/all_gather | solution.py:112
  7.9 246.2 %all-gather.8.cloned.1.call-start = ((), (), s32[]{:S(2)}) async-start(), calls=%async_computation.14 | async-start | bytes 9953280 | tf_op jit(solution)/shard_map/all_gather | solution.py:113
  8.7 432.2 %all-gather.10.cloned.1.call-start = ((), (), s32[]{:S(2)}) async-start(), calls=%async_computation.15 | async-start | bytes 3317760 | tf_op jit(solution)/shard_map/all_gather | solution.py:114
  9.4 102.0 %copy-start.57 = (bf16[1,272,1152]{2,1,0:T(8,128)(2,1)S(1)}, bf16[1,272,1152]{2,1,0:T(8,128)(2,1)}, u32[]{:S(2)}) copy-start(bf16[1,272,1152]{2,1,0:T(8,128)(2,1)} %param.22) | copy-start | bytes 1880068
  9.4 102.0 %copy-start.59 = (bf16[1,272,1152]{2,1,0:T(8,128)(2,1)S(1)}, bf16[1,272,1152]{2,1,0:T(8,128)(2,1)}, u32[]{:S(2)}) copy-start(bf16[1,272,1152]{2,1,0:T(8,128)(2,1)} %param.21) | copy-start | bytes 1880068
  9.5 536.5 %all-gather.12.cloned.1.call-start = ((), (), s32[]{:S(2)}) async-start(), calls=%async_computation.16 | async-start | bytes 13271040 | tf_op jit(solution)/shard_map/all_gather | solution.py:115
  10.0 722.7 %all-gather.14.cloned.1.call-start = ((), (), s32[]{:S(2)}) async-start(), calls=%async_computation.17 | async-start | bytes 13271040 | tf_op jit(solution)/shard_map/all_gather | solution.py:116
  10.6 243.5 %copy-start.27 = (f32[1152]{0:T(1024)}, f32[1152]{0:T(1024)S(1)}, u32[]{:S(2)}) copy-start(f32[1152]{0:T(1024)S(1)} %convert_element_type.139) | copy-start | bytes 13828
  10.7 243.4 %copy-start.46 = (f32[1152]{0:T(1024)}, f32[1152]{0:T(1024)S(1)}, u32[]{:S(2)}) copy-start(f32[1152]{0:T(1024)S(1)} %convert_element_type.140) | copy-start | bytes 13828
  115.9 144.2 %copy-start.2 = (f32[272,1152]{1,0:T(8,128)}, f32[272,1152]{1,0:T(8,128)S(1)}, u32[]{:S(2)}) copy-start(f32[272,1152]{1,0:T(8,128)S(1)} %get-tuple-element.206) | copy-start | bytes 3760132
  115.9 144.2 %copy-start.32 = (f32[272]{0:T(512)}, f32[272]{0:T(512)S(1)}, u32[]{:S(2)}) copy-start(f32[272]{0:T(512)S(1)} %broadcast_multiply_fusion.1) | copy-start | bytes 3268
  116.9 143.3 %copy-start.40 = (f32[272]{0:T(512)}, f32[272]{0:T(512)S(1)}, u32[]{:S(2)}) copy-start(f32[272]{0:T(512)S(1)} %fusion.76) | copy-start | bytes 3268
  274.1 37.8 %all-to-all-start.2 = ((bf16[4,2,39168]{2,1,0:T(2,128)(2,1)}), bf16[4,2,39168]{2,1,0:T(2,128)(2,1)}, u32[]{:S(2)}, u32[]{:S(2)}) async-start(bf16[4,2,39168]{2,1,0:T(2,128)(2,1)} %reshape.212), calls=%async_computation.2 | async-start | bytes 1253376 | tf_op jit(solution)/shard_map/all_to_all | solution.py:134
  311.9 23.7 %all-to-all-start.1 = ((bf16[4,2,39168]{2,1,0:T(2,128)(2,1)}), bf16[4,2,39168]{2,1,0:T(2,128)(2,1)}, u32[]{:S(2)}, u32[]{:S(2)}) async-start(bf16[4,2,39168]{2,1,0:T(2,128)(2,1)} %reshape.210), calls=%async_computation.1 | async-start | bytes 1253376 | tf_op jit(solution)/shard_map/all_to_all | solution.py:133
  335.7 42.2 %all-to-all-start = ((bf16[4,2,39168]{2,1,0:T(2,128)(2,1)}), bf16[4,2,39168]{2,1,0:T(2,128)(2,1)}, u32[]{:S(2)}, u32[]{:S(2)}) async-start(bf16[4,2,39168]{2,1,0:T(2,128)(2,1)} %reshape.208), calls=%async_computation | async-start | bytes 1253376 | tf_op jit(solution)/shard_map/all_to_all | solution.py:135
  395.9 41.8 %all-to-all-start.3 = ((bf16[4,272,288]{2,1,0:T(8,128)(2,1)}), bf16[4,272,288]{2,1,0:T(8,128)(2,1)S(1)}, u32[]{:S(2)}, u32[]{:S(2)}) async-start(bf16[4,272,288]{2,1,0:T(8,128)(2,1)} %copy.93), calls=%async_computation.3 | async-start | bytes 1671168 | tf_op jit(solution)/shard_map/all_to_all | solution.py:156
  399.9 357.5 %copy-start.29 = (f32[1152]{0:T(1024)}, f32[1152]{0:T(1024)S(1)}, u32[]{:S(2)}) copy-start(f32[1152]{0:T(1024)S(1)} %convert_element_type.144) | copy-start | bytes 13828
  400.6 145.4 %copy-start.48 = (f32[1152]{0:T(1024)}, f32[1152]{0:T(1024)S(1)}, u32[]{:S(2)}) copy-start(f32[1152]{0:T(1024)S(1)} %convert_element_type.145) | copy-start | bytes 13828
  444.4 312.9 %copy-start.34 = (f32[272]{0:T(512)}, f32[272]{0:T(512)S(1)}, u32[]{:S(2)}) copy-start(f32[272]{0:T(512)S(1)} %broadcast_multiply_fusion) | copy-start | bytes 3268
  445.8 311.6 %copy-start.42 = (f32[272]{0:T(512)}, f32[272]{0:T(512)S(1)}, u32[]{:S(2)}) copy-start(f32[272]{0:T(512)S(1)} %fusion.77) | copy-start | bytes 3268
  445.8 286.9 %copy-start.17 = (bf16[1,272,1152]{2,1,0:T(8,128)(2,1)S(1)}, bf16[1,272,1152]{2,1,0:T(8,128)(2,1)}, u32[]{:S(2)}) copy-start(bf16[1,272,1152]{2,1,0:T(8,128)(2,1)} %param.24) | copy-start | bytes 1880068
  774.6 29.0 %all-to-all-start.4 = ((bf16[4,2,39168]{2,1,0:T(2,128)(2,1)}), bf16[4,2,39168]{2,1,0:T(2,128)(2,1)S(1)}, u32[]{:S(2)}, u32[]{:S(2)}) async-start(bf16[4,2,39168]{2,1,0:T(2,128)(2,1)} %reshape.214), calls=%async_computation.4 | async-start | bytes 1253376 | tf_op jit(solution)/shard_map/all_to_all | solution.py:193
  778.1 168.7 %reduce-scatter.10.cloned.1.call-start = ((), (), s32[]{:S(2)}) async-start(), calls=%async_computation.20 | async-start | bytes 3317760 | tf_op jit(solution)/shard_map/reduce_scatter | solution.py:229
  836.4 22.9 %copy-start.12 = (bf16[2,2,272,4,72]{2,4,3,1,0:T(8,128)(2,1)S(1)}, bf16[2,2,272,4,72]{2,4,3,1,0:T(8,128)(2,1)}, u32[]{:S(2)}) copy-start(bf16[2,2,272,4,72]{2,4,3,1,0:T(8,128)(2,1)} %get-tuple-element.111) | copy-start | bytes 1880068
  836.4 19.4 %all-to-all-start.5 = ((bf16[4,272,288]{2,1,0:T(8,128)(2,1)}), bf16[4,272,288]{2,1,0:T(8,128)(2,1)S(1)}, u32[]{:S(2)}, u32[]{:S(2)}) async-start(bf16[4,272,288]{2,1,0:T(8,128)(2,1)} %copy.98), calls=%async_computation.5 | async-start | bytes 1671168 | tf_op jit(solution)/shard_map/all_to_all | solution.py:202
  855.8 21.8 %all-to-all-start.7 = ((bf16[4,272,288]{2,1,0:T(8,128)(2,1)}), bf16[4,272,288]{2,1,0:T(8,128)(2,1)S(1)}, u32[]{:S(2)}, u32[]{:S(2)}) async-start(bf16[4,272,288]{2,1,0:T(8,128)(2,1)} %copy.102), calls=%async_computation.7 | async-start | bytes 1671168 | tf_op jit(solution)/shard_map/all_to_all | solution.py:204
  877.5 23.1 %all-to-all-start.6 = ((bf16[4,272,288]{2,1,0:T(8,128)(2,1)}), bf16[4,272,288]{2,1,0:T(8,128)(2,1)S(1)}, u32[]{:S(2)}, u32[]{:S(2)}) async-start(bf16[4,272,288]{2,1,0:T(8,128)(2,1)} %copy.100), calls=%async_computation.6 | async-start | bytes 1671168 | tf_op jit(solution)/shard_map/all_to_all | solution.py:203
  881.0 128.5 %reduce-scatter.6.cloned.1.call-start = ((), (), s32[]{:S(2)}) async-start(), calls=%async_computation.18 | async-start | bytes 6635520 | tf_op jit(solution)/shard_map/reduce_scatter | solution.py:223
  915.5 235.2 %reduce-scatter.8.cloned.1.call-start = ((), (), s32[]{:S(2)}) async-start(), calls=%async_computation.19 | async-start | bytes 9953280 | tf_op jit(solution)/shard_map/reduce_scatter | solution.py:226
  924.5 409.2 %reduce-scatter.12.cloned.1.call-start = ((), (), s32[]{:S(2)}) async-start(), calls=%async_computation.21 | async-start | bytes 13271040 | tf_op jit(solution)/shard_map/reduce_scatter | solution.py:232
  935.8 581.5 %reduce-scatter.14.cloned.1.call-start = ((), (), s32[]{:S(2)}) async-start(), calls=%async_computation.22 | async-start | bytes 13271040 | tf_op jit(solution)/shard_map/reduce_scatter | solution.py:235
  946.6 715.4 %all-reduce.4.cloned.1.call-start = ((), (), s32[]{:S(2)}) async-start(), calls=%async_computation.23 | async-start | bytes 18579456 | tf_op jit(solution)/shard_map/psum | solution.py:240
  (56 other events, 225.8 us)
Sparse Core Ops, SparseCore 0:
  9.6 101.8 all-gather.5
  113.0 141.0 all-gather.7
  255.7 75.7 all-gather.9
  332.9 213.0 all-gather.11
  547.4 185.2 all-gather.13
  782.7 55.5 reduce-scatter.9
  915.6 93.9 reduce-scatter.5
  1012.0 138.5 reduce-scatter.7
  1153.0 180.6 reduce-scatter.11
  1336.1 181.1 reduce-scatter.13
  1521.8 140.2 all-reduce.3
where the time goes:
time: 1690 us; the launch traced here: 1680 us
  waiting for transfers between devices  1320 us (78%)
  matrix products  130 us (8%)
  local copies, waits for them, and re-layouts  99.2 us (6%)
  other arithmetic  45.6 us (3%)
  blocking collectives  45.1 us (3%)
  starting transfers between devices  31.4 us (2%)
    reduce_scatter x1, waiting for transfers between devices, body(): lax.psum_scatter(reduce_grad.astype(jnp.bfloat16), 'seq', scatter_dimensi...  184 us
    reduce_scatter x1, waiting for transfers between devices, body(): lax.psum_scatter(expand_grad.astype(jnp.bfloat16), 'seq', scatter_dimensi...  183 us
    all_gather x1, waiting for transfers between devices, body(): lax.all_gather(reduce_weight, 'seq', axis=0, tiled=True)  168 us
    reduce_scatter x1, waiting for transfers between devices, body(): lax.psum_scatter(triple_part.astype(jnp.bfloat16), 'seq', scatter_dimensi...  141 us
    all_gather x1, waiting for transfers between devices, body(): lax.all_gather(triple_weight, 'seq', axis=0, tiled=True)  137 us
    all_gather x1, waiting for transfers between devices, body(): lax.all_gather(merge_weight, 'seq', axis=0, tiled=True)  101 us
    all_gather x1, waiting for transfers between devices, body(): lax.all_gather(expand_weight, 'seq', axis=0, tiled=True)  100 us
    psum x1, waiting for transfers between devices, body(): lax.psum(merge_rows.astype(jnp.bfloat16), 'dp').astype(jnp.float32)  84.5 us
  transfers between devices with their start and end apart: 19, of which 17 were waited for; matrix products, arithmetic and copies ran while one was open for 12% of the time, Pallas kernels for 0%

commit v1 on v0

v1 whole, which is shorter than its diff:
```python
import functools

import jax
import jax.numpy as jnp
from jax import lax
from jax.experimental import pallas as pl
from jax.experimental.pallas import tpu as pltpu
from jax.sharding import PartitionSpec as P

MESH = pl.DeviceIdType.MESH
HEADS = 16
EPS = 1e-05
NEGATIVE = -1e30
NB = 14
NP, SUB = 7, 3
Q = NP * SUB
AHEAD = 2
RING = 8
SLOTS = 3
VR = 16
READY = 5
LEAD = READY + 11
f32, bf16 = jnp.float32, jnp.bfloat16


def block_slices(refs):
    merge, triple, output, expand, reduce = refs
    R, C = output.shape
    out = []
    for j in range(merge.shape[0] // R): out.append(merge.at[pl.ds(j * R, R), :])
    for j in range(triple.shape[1] // C): out.append(triple.at[:, pl.ds(j * C, C)])
    out.append(output.at[:, :])
    for j in range(expand.shape[1] // C): out.append(expand.at[:, pl.ds(j * C, C)])
    for j in range(reduce.shape[0] // R): out.append(reduce.at[pl.ds(j * R, R), :])
    return out


def nn(a, b):
    return jnp.dot(a, b, preferred_element_type=f32)


def nt(a, b):
    return lax.dot_general(a, b, (((1,), (1,)), ((), ())), preferred_element_type=f32)


def tn(a, b):
    return lax.dot_general(a, b, (((0,), (0,)), ((), ())), preferred_element_type=f32)


HID, SKP, COT, NORMED, ATT, TWO, ACT, TRI, BR, TG, GR, EXP, PX, ATTG, OUT, PLACES = 0, 2, 4, 6, 8, 10, 12, 20, 23, 25, 31, 33, 37, 39, 40, 42
NN, NT, EXTRA, CAST, FETCH, NORM, NORM_BACK, GELU, GELU_BACK, ATTEND, ATTEND_BACK, ROWS, FULL = range(1, 14)


def op(mode, a=0, w=0, acc=0, e=0, wait=1, pre=None, post=None):
    pre, post = (0 if v is None else v + 1 for v in (pre, post))
    return mode + 16 * (a + 64 * (w + 32 * (acc + 2 * (e + 2 * (wait + 2 * (pre + 32 * post))))))


def plan():
    B = READY
    ops = [(0, op(EXTRA, 0)), (1, op(EXTRA, 1))]
    ops += [(B + 1, o) for o in (op(FETCH, 0), op(NN, HID, 0, pre=1), op(NN, SKP, 1, acc=1), op(NORM, 0))]
    for j in range(3):
        ops += [(B + 2 + j, o) for o in (op(NN, NORMED, 2 + j, pre=2 + j), op(CAST, TRI + j))]
    ops += [(B + 4, op(ATTEND, 0)), (B + 4, op(ATTEND, 1)), (B + 5, op(ATTEND, 2)), (B + 5, op(ATTEND, 3)), (B + 5, op(EXTRA, 2))]
    ops += [(B + 5, op(NN, ATT, 5, pre=5)), (B + 5, op(NORM, 1))]
    for i in range(4):
        ops += [(B + 6 + i, op(NN, TWO, 6 + i, pre=6 + i)), (B + 6 + i, op(GELU, i))]
    ops += [(B + 9, op(EXTRA, 3)), (B + 9, op(ROWS, 0)), (B + 10, op(ROWS, 1))]
    ops += [(B + 13, op(FETCH, 10 + i)) for i in range(3)]
    for i in range(4):
        ops += [(B + 13 + i // 2, o) for o in (
            op(NN, ACT + 2 * i, 10 + i, acc=int(i > 0)), op(NT, COT, 10 + i, e=1, wait=0, post=13 + i), op(GELU_BACK, i))]
    ops += [(B + 14, op(EXTRA, 4)), (B + 15, op(EXTRA, 5)), (B + 15, op(FULL, 0)), (B + 16, op(FULL, 1))]
    for i in range(4):
        ops += [(B + 16 + (i > 0), op(NT, EXP + i, 14 + i, acc=int(i > 0), post=17 + i))]
    ops += [(B + 17, op(NORM_BACK, 1)), (B + 18, op(NT, BR, 18, post=21)), (B + 18, op(CAST, ATTG))]
    ops += [(B + 18 + g // 2, op(ATTEND_BACK, g)) for g in range(4)]
    ops += [(B + 19, op(EXTRA, 6)), (B + 20, op(EXTRA, 7)), (B + 20, op(FULL, 2)), (B + 21, op(FULL, 3))]
    for j in range(3):
        ops += [(B + 22, op(NT, TG + 2 * j, 19 + j, acc=int(j > 0), post=22 + j if j < 2 else None))]
    ops += [(B + 23, op(NORM_BACK, 0)), (B + 24, op(EXTRA, 8)), (B + 24, op(ROWS, 2)), (B + 25, op(EXTRA, 9))]
    for i in range(2):
        ops += [(B + 25, op(NT, GR, 22 + i)), (B + 25, op(CAST, OUT + i))]
    ops += [(B + 25, op(EXTRA, 10))]
    ops += [(B + t, op(EXTRA, 11 + i)) for i, t in enumerate((26, 27, 28, 29, 32))]
    return ops


OPS = plan()
STARTS = [sum(t < tick for t, _ in OPS) for tick in range(LEAD + AHEAD + Q + 10)]
UNITS = [2, 6] + [4 * j for j in range(2, 10)] + [1 + 4 * s for s in range(4)] + [4 * j for j in (6, 7, 8, 9, 5, 2, 3, 4)] + [2, 6]


def lookup(values, i):
    total = jnp.int32(values[0])
    for k in range(1, len(values)):
        if values[k] != values[k - 1]:
            total = total + jnp.where(i >= k, values[k] - values[k - 1], 0)
    return total


def block_kernel(hid, skp, cot_in, mask_in, vec_in, wm, wt, wo, we, wr,
                 res, hgrad, sgrad, F, WV, G, D,
                 W, X, PR, XH, MID, E, INV, MASK, VEC, DB,
                 K, R1, R2, R3, O, VB,
                 loc, loc2, zs, zr, xs, xr, ys, yr, cs, cr, fsem, insem, es, er, dsem, osem,
                 ld, s1, r1, s2, r2, s3, r3, st, sf, rf, sc, rcv, vl, vs, vr, *, nz):
    dp = lax.axis_index("dp"); z = lax.axis_index("seq")
    c = dp % 2; x = (dp // 2) % 2; y = dp // 4
    xn = dp + 2 - 4 * x; yn = dp + 4 - 8 * y; cn = dp + 1 - 2 * c; co = 1 - c
    L, C = X.shape[1:]
    R = G.shape[2]
    scale = (C // HEADS) ** -0.5
    bar = pltpu.get_barrier_semaphore()
    for tgt in (xn, yn, cn):
        pl.semaphore_signal(bar, inc=1, device_id=(tgt, z), device_id_type=MESH)
    for d in range(1, nz):
        pl.semaphore_signal(bar, inc=1, device_id=(dp, (z + d) % nz), device_id_type=MESH)

    def rc(src, dst, ss, rs, dev):
        return pltpu.make_async_remote_copy(src_ref=src, dst_ref=dst, send_sem=ss, recv_sem=rs, device_id=dev, device_id_type=MESH)

    blocks = block_slices((wm, wt, wo, we, wr))
    room = SLOTS * 4
    def stage(j): return W.at[(j % room) // 4, j % 4]
    def load_in(j): return pltpu.make_async_copy(blocks[j], stage(j), loc.at[j])
    def load_out(j, slot): return pltpu.make_async_copy(slot, G.at[z, j], loc2.at[j])
    for j in range(min(room, NB)): load_in(j).start()
    inputs = [pltpu.make_async_copy(a, b, insem.at[i]) for i, (a, b) in enumerate(
        ((hid, X.at[HID]), (skp, X.at[SKP]), (cot_in, X.at[COT]), (mask_in, MASK), (vec_in, VEC)))]
    for cp in inputs: cp.start()
    for j in range(min(room, NB)):
        load_in(j).wait()
        load_out(j, stage(j)).start()
    for j in range(AHEAD + 2): load_out(j, stage(j)).wait()
    for j in range(room, NB):
        load_in(j).start()
    pl.semaphore_wait(bar, nz + 2)

    half = R // 2; third = half // 3
    base = half * c
    zp = ((x + y) % 2) * (2 - x)
    yp = 1 + y
    def reg(s, b, start, n):
        return G.at[s, b, pl.ds(pl.multiple_of(start, 16), n), :]
    def same(region, ss, rs, dev): return rc(region, region, ss, rs, dev)
    def zcopy(b, d, k):
        s = z - k if d == 0 else z + k
        return same(reg(s, b, base + third * zp, third), zs.at[b, d, k], zr.at[b, d, k], (dp, z + 1 if d == 0 else z - 1))
    def zsend_ok(d, k):
        return (z >= k) & (z < nz - 1) if d == 0 else (z + k <= nz - 1) & (z > 0)
    def zrecv_ok(d, k):
        return z >= k + 1 if d == 0 else z + 1 + k <= nz - 1
    def shard_in(d, k):
        return z - 1 - k if d == 0 else z + 1 + k
    def xcopy(b, s): return same(reg(s, b, base + third * zp, third), xs.at[b, s], xr.at[b, s], (xn, z))
    def ycopy(b, s): return same(reg(s, b, base + third * yp, third), ys.at[b, s], yr.at[b, s], (yn, z))
    def ccopy(b, s): return same(reg(s, b, base, half), cs.at[b, s], cr.at[b, s], (cn, z))
    def own(b):
        for d in (0, 1):
            @pl.when(zsend_ok(d, 0))
            def _(): zcopy(b, d, 0).start()
    def zarr(b, d, k):
        zcopy(b, d, k).wait_recv()
        if k + 1 < nz - 1:
            @pl.when(zsend_ok(d, k + 1))
            def _(): zcopy(b, d, k + 1).start()
        s = shard_in(d, k)
        xcopy(b, s).start()
        @pl.when((x + y) % 2 == 1)
        def _(): ycopy(b, s).start()
    def xarr(b, d, k):
        s = shard_in(d, k)
        xcopy(b, s).wait_recv()
        @pl.when((x + y) % 2 == 0)
        def _(): ycopy(b, s).start()
    def yarr(b, d, k):
        s = shard_in(d, k)
        ycopy(b, s).wait_recv()
        ccopy(b, s).start()
    def fin(b, d, k):
        s = shard_in(d, k)
        ccopy(b, s).wait()
        xcopy(b, s).wait_send()
        ycopy(b, s).wait_send()
    for j in range(AHEAD): own(j)
    def gather_tick(t):
        @pl.when(t < NB - AHEAD)
        def _():
            own(t + AHEAD)
        for off, fn in ((0, zarr), (1, xarr), (2, yarr), (3, fin)):
            for k in range(nz - 1):
                b = t - off - k
                @pl.when((b >= 0) & (b < NB))
                def _():
                    for d in (0, 1):
                        @pl.when(zrecv_ok(d, k))
                        def _(): fn(b, d, k)
                        if off == 3:
                            @pl.when(zsend_ok(d, k))
                            def _(): zcopy(b, d, k).wait_send()

    T = K.shape[2]
    def ring(q): return q % RING
    def typ(q, s): return (q + s) % 2
    def keep(q, s): return x + typ(q, s) * (y - x)
    def near(q, s): return xn + typ(q, s) * (yn - xn)
    def far(q, s): return yn + typ(q, s) * (xn - yn)
    def piece(q, h):
        return NP - 1 - q // SUB, pl.ds(pl.multiple_of(half * h + T * (q % SUB), 16), T)
    def load(q, s):
        p, rows = piece(q, keep(q, s))
        return pltpu.make_async_copy(D.at[s, p, rows], K.at[ring(q), s], ld.at[s, q])
    def first(q, s):
        p, rows = piece(q, 1 - keep(q, s))
        return rc(D.at[s, p, rows], R1.at[ring(q), s], s1.at[s, q], r1.at[s, q], (near(q, s), z))
    def up(q, s):
        return rc(K.at[ring(q), s], R2.at[ring(q), s], s2.at[s, q], r2.at[s, q], (dp, z + 1))
    def down(q, s):
        away = jnp.minimum(z - 1 - s, 1)
        slot = nz + away * (s - nz)
        return rc(K.at[ring(q), s], R2.at[ring(q), slot], s2.at[s, q], r2.at[slot, q], (dp, z - 1))
    def got(slot, q):
        return rc(K.at[ring(q), 0], R2.at[ring(q), slot], s2.at[0, q], r2.at[slot, q], (dp, z))
    def last(q):
        return rc(K.at[ring(q), z], R3.at[ring(q)], s3.at[q], r3.at[q], (far(q, z), z))
    def frow(q, h, cc):
        p, rows = piece(q, h)
        return F.at[2 * p + cc, rows]
    def keepf(q): return pltpu.make_async_copy(O.at[ring(q)], frow(q, keep(q, z), c), st.at[q])
    def spread(q): return rc(O.at[ring(q)], frow(q, keep(q, z), c), sf.at[q], rf.at[q], (near(q, z), z))
    def spread_in(q):
        r = frow(q, 1 - keep(q, z), c)
        return rc(r, r, sf.at[q], rf.at[q], (near(q, z), z))
    def cross(q): return rc(O.at[ring(q)], frow(q, keep(q, z), c), sc.at[0, q], rcv.at[0, q], (cn, z))
    def cross2(q):
        r = frow(q, 1 - keep(q, z), c)
        return rc(r, r, sc.at[1, q], rcv.at[1, q], (cn, z))
    def add(a, b): return (a.astype(f32) + b.astype(f32)).astype(bf16)
    def issue(q):
        for s in range(nz):
            first(q, s).start(); load(q, s).start()
    def start(q):
        for s in range(nz):
            load(q, s).wait(); first(q, s).wait_recv()
            K[ring(q), s] = add(K[ring(q), s], R1[ring(q), s])
            if s > 0:
                @pl.when(z == 0)
                def _(): up(q, s).start()
            if s < nz - 1:
                @pl.when(z == nz - 1)
                def _(): down(q, s).start()
    def hop(q, k):
        for s in range(nz):
            if s > k:
                @pl.when(z == k)
                def _():
                    got(s, q).wait_recv()
                    K[ring(q), s] = add(K[ring(q), s], R2[ring(q), s])
                    up(q, s).start()
            if s < nz - 1 - k:
                @pl.when(z == nz - 1 - k)
                def _():
                    got(s, q).wait_recv()
                    K[ring(q), s] = add(K[ring(q), s], R2[ring(q), s])
                    down(q, s).start()
    def arrive(q):
        @pl.when(z > 0)
        def _():
            got(z, q).wait_recv()
            K[ring(q), z] = add(K[ring(q), z], R2[ring(q), z])
        @pl.when(z < nz - 1)
        def _():
            got(nz, q).wait_recv()
            K[ring(q), z] = add(K[ring(q), z], R2[ring(q), nz])
        last(q).start()
    def final(q):
        last(q).wait_recv()
        O[ring(q)] = add(K[ring(q), z], R3[ring(q)])
        keepf(q).start(); spread(q).start(); cross(q).start()
    def relay(q):
        spread_in(q).wait_recv()
        cross2(q).start()
        for s in range(nz):
            first(q, s).wait_send()
            if s > 0:
                @pl.when(z < s)
                def _(): up(q, s).wait_send()
            if s < nz - 1:
                @pl.when(z > s)
                def _(): down(q, s).wait_send()
        last(q).wait_send()
    def drain(q):
        keepf(q).wait(); spread(q).wait_send()
        cross(q).wait_send(); cross(q).wait_recv(); cross2(q).wait_send(); cross2(q).wait_recv()
    steps = [(0, start)] + [(k, functools.partial(hop, k=k)) for k in range(1, nz - 1)] + [
        (nz - 1, arrive), (nz, final), (nz + 1, relay), (nz + 3, drain)]
    def sum_tick(t):
        @pl.when((t >= 0) & (t < Q))
        def _(): issue(t)
        for off, fn in steps:
            q = t - AHEAD - off
            @pl.when((q >= 0) & (q < Q))
            def _(): fn(q)

    devs = ((cn, z), (xn, z), (yn, z))
    def swap(i): return rc(VB.at[2 * i], VB.at[2 * i + 1], vs.at[i], vr.at[i], devs[i])
    def vstep(i):
        if i > 0:
            swap(i - 1).wait()
            VB[2 * i] = VB[2 * i - 2] + VB[2 * i - 1]
        if i < 3:
            swap(i).start()
    def line(d):
        return rc(VB.at[6], VB.at[6 + d], vs.at[2 + d], vr.at[2 + d], (dp, (z + d) % nz))
    def vline():
        vstep(3)
        for d in range(1, nz): line(d).start()
    def vend():
        for d in range(1, nz): line(d).wait()
        def plane(s): return VB[6 + (z - s + nz) % nz]
        total = plane(0)
        for s in range(1, nz): total = total + plane(s)
        VB[0] = total
        cp = pltpu.make_async_copy(VB.at[0], WV, vl.at[1])
        cp.start(); cp.wait()

    def pair(i, src, dst): return rc(src, dst, es.at[i], er.at[i], (cn, z))
    def both(i, a): return pair(i, X.at[a], X.at[a + 1])
    ex = {
        "hid": both(0, HID), "skp": both(1, SKP), "cot": both(2, COT), "normed": both(3, NORMED), "att": both(4, ATT), "two": both(5, TWO),
        "px0": pair(10, X.at[EXP + co], X.at[PX]), "px1": pair(11, X.at[EXP + co + 2], X.at[PX + 1]), "br": both(12, BR),
        "qk": both(13, TG + 2 * co), "v": both(14, TG + 4), "gr": both(15, GR),
    }
    def qk_in(): return both(13, TG + 2 * c)
    def send_act(i): return both(6 + i, ACT + 2 * i)
    def arrived(*names):
        for n in names: ex[n].wait()

    def fetch(n):
        code = lookup(UNITS, n)
        kind, arg = code % 4, code // 4
        for i in range(4):
            s = jnp.where(kind == 0, i, jnp.where(kind == 1, arg, 2 * arg + i // 2))
            j = jnp.where(kind == 0, arg, jnp.where(kind == 1, 10 + i, i % 2))
            pltpu.make_async_copy(G.at[s, j], W.at[n % SLOTS, i], fsem.at[n % SLOTS, i]).start()
    def fetched(n):
        for i in range(4):
            pltpu.make_async_copy(G.at[0, 0], W.at[n % SLOTS, i], fsem.at[n % SLOTS, i]).wait()
    def weight(n): return W[n % SLOTS].reshape(4 * R, C)
    def vec(i): return VEC[pl.ds(i, 1), :]
    def tally(i, v): VB[0, pl.ds(i, 1), :] = jnp.sum(v, axis=0, keepdims=True)

    def do_matmul(dot, a, n, acc, e, wait, pre, post):
        @pl.when(pre > 0)
        def _(): fetch(pre - 1)
        @pl.when(wait > 0)
        def _(): fetched(n)
        v = dot(X[a], weight(n))
        E[e] = jnp.where(acc > 0, E[e], 0.0) + v
        @pl.when(post > 0)
        def _(): fetch(post - 1)
    def do_cast(a):
        X[a] = E[0].astype(bf16)
    def do_norm(k):
        v = jnp.where(k > 0, MID[...], 0.0) + E[0] + vec(3 * k)
        MID[...] = v
        m = v - jnp.mean(v, axis=-1, keepdims=True)
        r = lax.rsqrt(jnp.mean(m * m, axis=-1, keepdims=True) + EPS)
        XH[k] = m * r
        INV[k] = jnp.broadcast_to(r, INV.shape[1:])
        a = NORMED + (TWO - NORMED) * k
        X[a] = (m * r * vec(3 * k + 1) + vec(3 * k + 2)).astype(bf16)
        both(3 + 2 * k, a).start()
    def do_norm_back(k):
        e = E[0]
        xhat = XH[k]
        tally(3 * k + 1, e * xhat); tally(3 * k + 2, e)
        t = e * vec(3 * k + 1)
        a = jnp.mean(t, axis=-1, keepdims=True)
        b = jnp.mean(t * xhat, axis=-1, keepdims=True)
        v = MID[...] + (t - a - xhat * b) * INV[k, :, 0:1]
        MID[...] = v
        low = v.astype(bf16)
        a = GR + (BR - GR) * k
        X[a] = low
        tally(3 * k, low.astype(f32))
        both(15 - 3 * k, a).start()
    step = C // 3
    def part(n): return pl.ds(pl.multiple_of(step * n, 128), step)
    def do_gelu(i):
        def one(n, _):
            v = E[0, :, part(n)] + VEC[pl.ds(7 + i, 1), part(n)]
            cdf = 0.5 * (1.0 + lax.erf(v * (0.5 ** 0.5)))
            X[ACT + 2 * i, :, part(n)] = (v * cdf).astype(bf16)
            X[EXP + i, :, part(n)] = (cdf + v * jnp.exp(-0.5 * v * v) * 0.3989422804014327).astype(bf16)
            return 0
        lax.fori_loop(0, 3, one, 0)
        send_act(i).start()
    def do_gelu_back(i):
        def one(n, _):
            low = (E[1, :, part(n)] * X[EXP + i, :, part(n)].astype(f32)).astype(bf16)
            X[EXP + i, :, part(n)] = low
            VB[0, pl.ds(7 + i, 1), part(n)] = jnp.sum(low.astype(f32), axis=0, keepdims=True)
            return 0
        lax.fori_loop(0, 3, one, 0)
    hs = C // HEADS
    group = HEADS // 4
    def do_attend(i):
        for g in range(4):
            @pl.when(i == g)
            def _():
                for h in range(group * g, group * g + group):
                    sl = slice(hs * h, hs * h + hs)
                    scores = nt(X[TRI + 1, :, sl], X[TRI, :, sl]) * scale
                    scores = jnp.where(MASK[:, 0:1] > 0, scores, NEGATIVE)
                    e = jnp.exp(scores - jnp.max(scores, axis=0, keepdims=True))
                    p = (e * (1.0 / jnp.sum(e, axis=0, keepdims=True))).astype(bf16)
                    PR[h] = p
                    X[ATT, :, sl] = tn(p, X[TRI + 2, :, sl]).astype(bf16)
    def do_attend_back(i):
        for g in range(4):
            @pl.when(i == g)
            def _():
                for h in range(group * g, group * g + group):
                    sl = slice(hs * h, hs * h + hs)
                    q, k, v, d, p = X[TRI, :, sl], X[TRI + 1, :, sl], X[TRI + 2, :, sl], X[ATTG, :, sl], PR[h]
                    X[TG + 4, :, sl] = nn(p, d).astype(bf16)
                    pg = nt(v, d)
                    pf = p.astype(f32)
                    sg = (pf * (pg - jnp.sum(pf * pg, axis=0, keepdims=True))).astype(bf16)
                    X[TG, :, sl] = (tn(sg, k) * scale).astype(bf16)
                    X[TG + 2, :, sl] = (nn(sg, q) * scale).astype(bf16)
    def put(p):
        cps = [pltpu.make_async_copy(DB.at[pl.ds(R * s, R)], D.at[s, p], dsem.at[s]) for s in range(4)]
        for cp in cps: cp.start()
        for cp in cps: cp.wait()
    def do_rows(kind):
        merge = kind // 2
        right = COT + (GR - COT) * merge
        def one(s, _):
            left = ACT + 2 * s + merge * (HID + 2 * (s // 2) - ACT - 2 * s)
            cut = merge * (2 * (s % 2)) + (1 - merge) * 2 * (1 - kind) + c
            rows = pl.ds(pl.multiple_of(R * s, 16), R)
            for v in range(4):
                @pl.when(cut == v)
                def _():
                    sl = slice(R * v, R * v + R)
                    DB[rows] = (tn(X[left, :, sl], X[right]) + tn(X[left + 1, :, sl], X[right + 1])).astype(bf16)
            return 0
        lax.fori_loop(0, 4, one, 0)
        put(6 - kind - 4 * merge)
    def do_full(kind):
        left = jnp.where(kind < 2, TWO, jnp.where(kind == 2, NORMED + (ATT - NORMED) * c, NORMED))
        right = jnp.where(kind == 0, EXP + 2 + c, jnp.where(kind == 1, EXP + c, jnp.where(kind == 2, TG + 4 + (BR - TG - 4) * c, TG + 2 * c)))
        other = jnp.where(kind == 0, PX + 1, jnp.where(kind == 1, PX, right + 1))
        def one(n, _):
            DB[pl.ds(pl.multiple_of(step * n, 128), step)] = (tn(X[left, :, part(n)], X[right]) + tn(X[left + 1, :, part(n)], X[other])).astype(bf16)
            return 0
        lax.fori_loop(0, 3, one, 0)
        put(4 - kind)

    def x_begin():
        VB[0] = jnp.zeros_like(VB[0])
        for cp in inputs: cp.wait()
        for n in ("hid", "skp", "cot"): ex[n].start()
        for j in range(room, NB):
            load_in(j).wait()
            load_out(j, stage(j)).start()
    def x_stored():
        for j in range(AHEAD + 2, NB): load_out(j, stage(j)).wait()
    def x_attended(): ex["att"].start()
    def x_acts():
        arrived("cot")
        for i in range(4): send_act(i).wait()
    def x_result():
        ex["px0"].start(); ex["px1"].start()
        X[OUT] = (MID[...] + E[0] + vec(6)).astype(bf16)
        pltpu.make_async_copy(X.at[OUT], res, osem.at[0]).start()
        up_ = X[COT].astype(f32)
        MID[...] = up_
        tally(6, up_)
    def x_px(): arrived("px0", "px1", "two")
    def x_triple():
        ex["qk"].start(); ex["v"].start()
    def x_heads():
        arrived("normed", "att", "br", "v")
        ex["qk"].wait_send(); qk_in().wait_recv()
    def x_merge(): arrived("hid", "skp", "gr")
    def x_outs():
        pltpu.make_async_copy(X.at[OUT], res, osem.at[0]).wait()
    def x_last():
        outs = [pltpu.make_async_copy(X.at[OUT + i], (hgrad, sgrad)[i], osem.at[1 + i]) for i in range(2)]
        for cp in outs: cp.start()
        for cp in outs: cp.wait()
    extras = [x_begin, x_stored, x_attended, x_acts, x_result, x_px, x_triple, x_heads, x_merge, x_outs, x_last,
              functools.partial(vstep, 0), functools.partial(vstep, 1), functools.partial(vstep, 2), vline, vend]
    def do_extra(i):
        for k, fn in enumerate(extras):
            @pl.when(i == k)
            def _(): fn()

    def run(n, _):
        code = lookup([op for _, op in OPS], n)
        mode, a, w = code % 16, code // 16 % 64, code // 1024 % 32
        acc, e, wait = code // 2 ** 15 % 2, code // 2 ** 16 % 2, code // 2 ** 17 % 2
        pre, post = code // 2 ** 18 % 32, code // 2 ** 23 % 32
        small = ((do_extra, EXTRA), (do_cast, CAST), (fetch, FETCH), (do_norm, NORM), (do_norm_back, NORM_BACK), (do_gelu, GELU),
                 (do_gelu_back, GELU_BACK), (do_attend, ATTEND), (do_attend_back, ATTEND_BACK), (do_rows, ROWS), (do_full, FULL))
        for dot, m in ((nn, NN), (nt, NT)):
            @pl.when(mode == m)
            def _(): do_matmul(dot, a, w, acc, e, wait, pre, post)
        for fn, m in small:
            @pl.when(mode == m)
            def _(): fn(a)
        return 0

    def tick(t, _):
        @pl.when(t < NB + nz - 2 + 3)
        def _(): gather_tick(t)
        @pl.when(t >= LEAD)
        def _(): sum_tick(t - LEAD)
        lax.fori_loop(lookup(STARTS, t), lookup(STARTS, t + 1), run, 0)
        return 0
    lax.fori_loop(0, LEAD + AHEAD + Q + nz + 3, tick, 0)


def block(hidden, skipped, cotangent, mask, vectors, weights, nz):
    L, C = hidden.shape
    R = weights[2].shape[0]
    T = R // 2 // SUB
    S = pltpu.SemaphoreType.DMA
    V = pltpu.VMEM
    rows = jax.ShapeDtypeStruct((L, C), bf16)
    hbm = pl.BlockSpec(memory_space=pl.ANY)
    out_shape = (rows, rows, rows, jax.ShapeDtypeStruct((NB, R, C), bf16), jax.ShapeDtypeStruct((VR, C), f32),
                 jax.ShapeDtypeStruct((nz, NB, R, C), bf16), jax.ShapeDtypeStruct((nz, NP, R, C), bf16))
    scratch = [
        V((SLOTS, 4, R, C), bf16), V((PLACES, L, C), bf16), V((HEADS, L, L), bf16), V((2, L, C), f32), V((L, C), f32),
        V((2, L, C), f32), V((2, L, 128), f32), V((L, 128), f32), V((VR, C), f32), V((4 * R, C), bf16),
        V((RING, nz, T, C), bf16), V((RING, nz, T, C), bf16), V((RING, nz + 1, T, C), bf16), V((RING, T, C), bf16), V((RING, T, C), bf16),
        V((6 + nz, VR, C), f32),
        S((NB,)), S((NB,)), S((NB, 2, nz - 1)), S((NB, 2, nz - 1)), S((NB, nz)), S((NB, nz)), S((NB, nz)), S((NB, nz)), S((NB, nz)), S((NB, nz)),
        S((SLOTS, 4)), S((5,)), S((16,)), S((16,)), S((4,)), S((3,)),
        S((nz, Q)), S((nz, Q)), S((nz, Q)), S((nz, Q)), S((nz + 1, Q)), S((Q,)), S((Q,)), S((Q,)), S((Q,)), S((Q,)), S((2, Q)), S((2, Q)),
        S((2,)), S((2 + nz,)), S((2 + nz,)),
    ]
    return pl.pallas_call(
        functools.partial(block_kernel, nz=nz),
        out_shape=out_shape, in_specs=[hbm] * 10, out_specs=(hbm,) * 7, scratch_shapes=scratch,
        compiler_params=pltpu.CompilerParams(collective_id=0, has_side_effects=True, vmem_limit_bytes=63 * 2**20),
    )(hidden, skipped, cotangent, mask, vectors, *weights)[:5]


def unpack_kernel(F, m, t, o, e, r):
    i = pl.program_id(0)
    for out, lo, n in ((m, 0, 2), (t, 2, 3), (o, 5, 1), (e, 6, 4), (r, 10, 4)):
        @pl.when((i >= lo) & (i < lo + n))
        def _(): out[...] = F[0].astype(f32)


def unpack(F):
    R, C = F.shape[1:]
    def spot(lo, n, along):
        def index(i):
            j = jnp.clip(i - lo, 0, n - 1)
            return (j, 0) if along == 0 else (0, j)
        return pl.BlockSpec((R, C), index)
    shapes = [(2 * R, C), (R, 3 * C), (R, C), (R, 4 * C), (4 * R, C)]
    return pl.pallas_call(
        unpack_kernel, grid=(NB,),
        out_shape=[jax.ShapeDtypeStruct(s, f32) for s in shapes],
        in_specs=[pl.BlockSpec((1, R, C), lambda i: (i, 0, 0))],
        out_specs=[spot(0, 2, 0), spot(2, 3, 1), spot(5, 1, 0), spot(6, 4, 1), spot(10, 4, 0)],
        compiler_params=pltpu.CompilerParams(vmem_limit_bytes=48 * 2**20),
    )(F)

def pack(m, t, o, e, r):
    R, C = o.shape
    def cut(w):
        a, b = w.shape
        return w.reshape(a // R, R, b // C, C).transpose(0, 2, 1, 3).reshape(-1, R, C)
    return jnp.concatenate([cut(w) for w in (m, t, o, e, r)])


def against(left, right):
    return lax.dot_general(left, right, (((1,), (1,)), ((), ())), preferred_element_type=jnp.float32)


def weight_grad(left, right):
    return lax.dot_general(left, right, (((0,), (0,)), ((), ())), preferred_element_type=jnp.float32)


def norm_parts(v):
    c = v - jnp.mean(v, axis=-1, keepdims=True)
    inv = lax.rsqrt(jnp.mean(c * c, axis=-1, keepdims=True) + EPS)
    return c * inv, inv


def norm_back(e, xhat, inv, gain):
    t = e * gain
    return (t - jnp.mean(t, axis=-1, keepdims=True) - xhat * jnp.mean(t * xhat, axis=-1, keepdims=True)) * inv


def plain(hidden, skipped, row_mask, cotangent, merge_weight, merge_bias, first_gain, first_shift, triple_weight,
         output_weight, output_bias, second_gain, second_shift, expand_weight, expand_bias, reduce_weight, reduce_bias):
    length, D = hidden.shape[1:]
    hs = D // HEADS
    nz = lax.axis_size("seq")
    z = lax.axis_index("seq")
    c = lax.axis_index("dp") % 2
    weights = (merge_weight, triple_weight, output_weight, expand_weight, reduce_weight)
    G = lax.all_gather(pack(*weights), "seq")
    R = G.shape[2]
    merge_full = G[:, 0:2].reshape(2 * D, D)
    triple_full = G[:, 2:5].transpose(1, 0, 2, 3).reshape(3, D, D)
    output_full = G[:, 5].reshape(D, D)
    expand_full = G[:, 6:10].transpose(1, 0, 2, 3).reshape(4, D, D)
    reduce_full = G[:, 10:14].reshape(4 * D, D)
    gain_a, shift_a, gain_b, shift_b = (v.astype(f32) for v in (first_gain, first_shift, second_gain, second_shift))
    joined = jnp.concatenate([hidden[0], skipped[0]], axis=-1)
    merged = jnp.dot(joined, merge_full, preferred_element_type=f32) + merge_bias.astype(f32)
    xhat_a, inv_a = norm_parts(merged)
    normed = (xhat_a * gain_a + shift_a).astype(bf16)
    triple = jnp.einsum("ld,jde->jle", normed, triple_full, preferred_element_type=f32).astype(bf16)
    queries, key_heads, value_heads = (triple[j].reshape(length, HEADS, hs) for j in range(3))
    valid = lax.dynamic_index_in_dim(row_mask, z, 0, False)
    scores = jnp.einsum("qhd,khd->hqk", queries, key_heads, preferred_element_type=f32) * hs ** -0.5
    scores = jnp.where(valid[None, None, :] > 0, scores, NEGATIVE)
    weights_ = jnp.exp(scores - jnp.max(scores, axis=-1, keepdims=True))
    probs = weights_ / jnp.sum(weights_, axis=-1, keepdims=True)
    probs_low = probs.astype(bf16)
    attended = jnp.einsum("hqk,khd->qhd", probs_low, value_heads, preferred_element_type=f32).astype(bf16).reshape(length, D)
    middle = merged + jnp.dot(attended, output_full, preferred_element_type=f32) + output_bias.astype(f32)
    xhat_b, inv_b = norm_parts(middle)
    normed_two = (xhat_b * gain_b + shift_b).astype(bf16)
    expanded = jnp.einsum("ld,jde->jle", normed_two, expand_full, preferred_element_type=f32) + expand_bias.astype(f32).reshape(4, 1, D)
    activated, gelu_back = jax.vjp(functools.partial(jax.nn.gelu, approximate=False), expanded)
    activated = activated.astype(bf16).transpose(1, 0, 2).reshape(length, 4 * D)
    result = middle + jnp.dot(activated, reduce_full, preferred_element_type=f32) + reduce_bias.astype(f32)
    result = result.astype(bf16)
    upstream = cotangent[0]
    wide = upstream.astype(f32)
    activated_grad = jnp.einsum("le,jde->jld", upstream, reduce_full.reshape(4, D, D), preferred_element_type=f32)
    expanded_grad = gelu_back(activated_grad)[0].astype(bf16)
    e_two = jnp.einsum("jle,jde->ld", expanded_grad, expand_full, preferred_element_type=f32)
    middle_grad = wide + norm_back(e_two, xhat_b, inv_b, gain_b)
    branch_grad = middle_grad.astype(bf16)
    attended_grad = against(branch_grad, output_full).astype(bf16).reshape(length, HEADS, hs)
    prob_grad = jnp.einsum("qhd,khd->hqk", attended_grad, value_heads, preferred_element_type=f32)
    values_grad = jnp.einsum("hqk,qhd->khd", probs_low, attended_grad, preferred_element_type=f32)
    score_grad = (probs * (prob_grad - jnp.sum(probs * prob_grad, axis=-1, keepdims=True))).astype(bf16)
    queries_grad = jnp.einsum("hqk,khd->qhd", score_grad, key_heads, preferred_element_type=f32) * hs ** -0.5
    keys_grad = jnp.einsum("hqk,qhd->khd", score_grad, queries, preferred_element_type=f32) * hs ** -0.5
    triple_grad = jnp.stack([g.astype(bf16).reshape(length, D) for g in (queries_grad, keys_grad, values_grad)])
    e_one = jnp.einsum("jle,jde->ld", triple_grad, triple_full, preferred_element_type=f32)
    merged_grad = (middle_grad + norm_back(e_one, xhat_a, inv_a, gain_a)).astype(bf16)
    joined_grad = against(merged_grad, merge_full).astype(bf16)
    vectors = jnp.stack([
        jnp.sum(merged_grad.astype(f32), 0), jnp.sum(e_one * xhat_a, 0), jnp.sum(e_one, 0),
        jnp.sum(branch_grad.astype(f32), 0), jnp.sum(e_two * xhat_b, 0), jnp.sum(e_two, 0), jnp.sum(wide, 0),
    ])
    vectors = jnp.concatenate([vectors, jnp.sum(expanded_grad.astype(f32), 1), jnp.zeros((VR - 11, D), f32)])

    count = lax.axis_size("dp")
    def both(v):
        other = lax.ppermute(v, "dp", [(i, i + 1 - 2 * (i % 2)) for i in range(count)])
        return jnp.concatenate([v, other], axis=-2)
    joined2, normed2, triple2, attended2, branch2, normed_two2, expanded2, activated2, upstream2 = (
        both(v) for v in (joined, normed, triple_grad, attended, branch_grad, normed_two, expanded_grad, activated, upstream))
    def pick(v, axis, index):
        return lax.dynamic_index_in_dim(v, index, axis, False)
    def rows(left, right):
        return jnp.einsum("lsr,le->sre", left, right, preferred_element_type=f32).astype(bf16)
    def split(left):
        return left.reshape(left.shape[0], nz, -1, R)
    parts = [
        rows(pick(split(joined2), 2, c), both(merged_grad)),
        rows(split(normed2)[:, :, 0], pick(triple2, 0, c)),
        rows(split(jnp.where(c == 0, normed2, attended2))[:, :, 0], jnp.where(c == 0, triple2[2], branch2)),
        rows(split(normed_two2)[:, :, 0], pick(expanded2, 0, c)),
        rows(split(normed_two2)[:, :, 0], pick(expanded2, 0, c + 2)),
        rows(pick(split(activated2), 2, c), upstream2),
        rows(pick(split(activated2), 2, c + 2), upstream2),
    ]
    grads = jnp.stack(parts, axis=1)
    wide_grads = jnp.stack([jnp.where(c == i, grads, 0) for i in range(2)], axis=2).reshape(nz, NB, R, D)
    F = lax.psum(lax.psum_scatter(wide_grads, "seq", scatter_dimension=0, tiled=False), "dp")
    vectors = lax.psum(vectors, ("dp", "seq"))
    F = F.astype(f32)
    def columns(blocks):
        return blocks.transpose(1, 0, 2).reshape(R, -1)
    summed = (F[0:2].reshape(-1, D), columns(F[2:5]), F[5], columns(F[6:10]), F[10:14].reshape(-1, D))
    return outputs((result, joined_grad[:, :D], joined_grad[:, D:]), summed, vectors)


def outputs(images, summed, vectors):
    result, hidden_grad, skipped_grad = images
    merge, triple, output, expand, reduce = summed
    return (result[None], hidden_grad[None], skipped_grad[None], merge, vectors[0], vectors[1], vectors[2], triple, output,
            vectors[3], vectors[4], vectors[5], expand, vectors[7:11].reshape(-1), reduce, vectors[6])


def body(hidden, skipped, row_mask, cotangent, merge_weight, merge_bias, first_gain, first_shift, triple_weight,
         output_weight, output_bias, second_gain, second_shift, expand_weight, expand_bias, reduce_weight, reduce_bias):
    L, C = hidden.shape[1:]
    nz = lax.axis_size("seq")
    valid = lax.dynamic_index_in_dim(row_mask, lax.axis_index("seq"), 0, False)
    mask = jnp.broadcast_to(valid.astype(f32)[:, None], (L, 128))
    vectors = jnp.concatenate([
        merge_bias, first_gain, first_shift, output_bias, second_gain, second_shift, reduce_bias, expand_bias,
        jnp.zeros(((VR - 11) * C,), bf16)]).astype(f32).reshape(VR, C)
    weights = (merge_weight, triple_weight, output_weight, expand_weight, reduce_weight)
    *images, F, sums = block(hidden[0], skipped[0], cotangent[0], mask, vectors, weights, nz)
    return outputs(images, unpack(F), sums)


def solution(mesh):
    rows, held, copied = P(("dp", "seq"), None, None), P("seq", None), P()
    fast = mesh.shape["dp"] == 8 and mesh.shape["seq"] == 4
    return jax.shard_map(
        body if fast else plain,
        mesh=mesh,
        in_specs=(rows, rows, P("dp", None), rows, held, copied, copied, copied, held, held, copied, copied, copied,
                  held, copied, held, copied),
        out_specs=(rows, rows, rows, held, copied, copied, copied, held, held, copied, copied, copied, held, copied,
                   held, copied),
        check_vma=False,
    )
```

time: 1690 us -> 370 us (0.22)
  waiting for transfers between devices: 1320 us -> 0 us
  Pallas kernels: 0 us -> 353 us
  matrix products: 130 us -> 0 us
  local copies, waits for them, and re-layouts: 99.2 us -> 14.7 us
  blocking collectives: 45.1 us -> 0 us
  other arithmetic: 45.6 us -> 0.72 us
  starting transfers between devices: 31.4 us -> 0 us
    reduce_scatter x5 -> x0, waiting for transfers between devices: 571 us -> none  [the longest x1 184 us: body(): lax.psum_scatter(reduce_grad.astype(jnp.bfloat16), 'seq', scatter_dimensi...]
    all_gather x5 -> x0, waiting for transfers between devices: 506 us -> none  [the longest x1 168 us: body(): lax.all_gather(reduce_weight, 'seq', axis=0, tiled=True)]
    pallas_call x0 -> x2, Pallas kernels: none -> 353 us  [the longest x1 338 us: block(): pl.pallas_call(functools.partial(block_kernel, nz=nz), out_shape=out_shap...]
    all_to_all x8 -> x0, waiting for transfers between devices: 151 us -> none  [the longest x1 35.8 us: body(): lax.all_to_all(attended_heads, 'seq', split_axis=0, concat_axis=2, tiled=...]
    dot_general x29 -> x0, matrix products: 130 us -> none  [the longest x5 38.3 us: weight_grad(): lax.dot_general(left, right, (((0,), (0,)), ((), ())), preferred_element_...]
    psum x1 -> x0, waiting for transfers between devices: 84.5 us -> none  [body(): lax.psum(merge_rows.astype(jnp.bfloat16), 'dp').astype(jnp.float32)]
    psum x1 -> x0, blocking collectives: 45.1 us -> none  [body(): lax.psum((merge_bias_part, gain_a_part, shift_a_part, output_bias_part, g...]
    all_to_all x19 -> x0, local copies, waits for them, and re-layouts: 32.5 us -> none  [the longest x3 8.52 us: body(): lax.all_to_all(attended_grad, 'seq', split_axis=2, concat_axis=0, tiled=T...]
  transfers between devices with their start and end apart: 19 -> 0, of which waited for: 17 -> 0; matrix products, arithmetic and copies ran while one was open for 12% -> 0% of each run, Pallas kernels for 0% -> 0%
where the time goes in v1:
time: 370 us; the launch traced here: 369 us
  Pallas kernels  353 us (95%)
  local copies, waits for them, and re-layouts  14.7 us (4%)
    pallas_call x1, Pallas kernels, block(): pl.pallas_call(functools.partial(block_kernel, nz=nz), out_shape=out_shap...  338 us
    pallas_call x1, Pallas kernels, unpack(): pl.pallas_call(unpack_kernel, grid=(NB,), out_shape=[jax.ShapeDtypeStruct...  14.9 us
    unnamed x17, local copies, waits for them, and re-layouts  9.57 us

profile of v1, /device:TPU:0, one launch (start us, length us, event | category | flops | bytes accessed | tf_op | source)
XLA Modules:
  0.0 368.8 jit_solution(8002000114168082299)
XLA Ops:
  0.6 0.7 convert_reduce_fusion
  1.4 0.9 dynamic-update-slice
  2.3 0.9 dynamic-update-slice.1
  3.1 0.9 dynamic-update-slice.2
  4.0 0.9 dynamic-update-slice.3
  4.9 0.9 dynamic-update-slice.4
  5.8 0.9 dynamic-update-slice.5
  6.6 0.9 dynamic-update-slice.6
  7.5 0.9 dynamic-update-slice.7
  8.5 0.3 dynamic-update-slice.8
  8.8 0.7 reshape.46.vec_in
  9.5 0.8 broadcast_in_dim.18.mask_in
  10.3 337.8 %shard_map.288 = (bf16[272,1152]{1,0:T(8,128)(2,1)}, bf16[272,1152]{1,0:T(8,128)(2,1)}, bf16[272,1152]{1,0:T(8,128)(2,1)}, bf16[14,288,1152]{2,1,0:T(8,128)(2,1)...) custom-call(bf16[272,1152]{1,0:T(8,128)(2,1)} %bitcast.9, ...), custom_call_target="tpu_custom_call" | custom-call | tf_op jit(solution)/shard_map/pallas_call | solution.py:549
  348.1 0.9 slice.30
  348.9 1.9 slice_reduce_fusion
  350.8 0.6 reshape.45
  351.4 0.0 copy-start.2
  351.4 0.0 copy-start.1
  351.4 0.0 copy-start
  351.4 14.9 %shard_map.289 = (f32[576,1152]{1,0:T(8,128)}, f32[288,3456]{1,0:T(8,128)}, f32[288,1152]{1,0:T(8,128)}, f32[288,4608]{1,0:T(8,128)}, f32[1152,1152]{1,0:T(8,128)}) custom-call(bf16[14,288,1152]{2,1,0:T(8,128)(2,1)} %get-tuple-element.29.F), custom_call_target="tpu_custom_call" | custom-call | tf_op jit(solution)/shard_map/pallas_call | solution.py:571
  366.4 0.0 copy-done.2
  366.4 0.8 copy.45
  367.2 0.0 copy-done.1
  367.2 0.8 copy.46
  368.0 0.0 copy-done
  368.0 0.8 copy.47
  (2 shorter events, 0.0 us)
Async XLA Ops:
  351.4 14.9 %copy-start.2 = (bf16[272,1152]{1,0:T(8,128)(2,1)S(1)}, bf16[272,1152]{1,0:T(8,128)(2,1)}, u32[]{:S(2)}) copy-start(bf16[272,1152]{1,0:T(8,128)(2,1)} %get-tuple-element.26) | copy-start | bytes 1880068
  351.4 15.7 %copy-start.1 = (bf16[272,1152]{1,0:T(8,128)(2,1)S(1)}, bf16[272,1152]{1,0:T(8,128)(2,1)}, u32[]{:S(2)}) copy-start(bf16[272,1152]{1,0:T(8,128)(2,1)} %get-tuple-element.27) | copy-start | bytes 1880068
  351.4 16.6 %copy-start = (bf16[272,1152]{1,0:T(8,128)(2,1)S(1)}, bf16[272,1152]{1,0:T(8,128)(2,1)}, u32[]{:S(2)}) copy-start(bf16[272,1152]{1,0:T(8,128)(2,1)} %get-tuple-element.28) | copy-start | bytes 1880068

commit v2 on v1

--- a/solution.py
+++ b/solution.py
@@ -19,7 +19,7 @@
 SLOTS = 3
 VR = 16
 READY = 5
-LEAD = READY + 11
+LEAD = READY + 10
 f32, bf16 = jnp.float32, jnp.bfloat16
 
 
@@ -100,12 +100,13 @@
     return total
 
 
-def block_kernel(hid, skp, cot_in, mask_in, vec_in, wm, wt, wo, we, wr,
-                 res, hgrad, sgrad, F, WV, G, D,
-                 W, X, PR, XH, MID, E, INV, MASK, VEC, DB,
-                 K, R1, R2, R3, O, VB,
-                 loc, loc2, zs, zr, xs, xr, ys, yr, cs, cr, fsem, insem, es, er, dsem, osem,
-                 ld, s1, r1, s2, r2, s3, r3, st, sf, rf, sc, rcv, vl, vs, vr, *, nz):
+def block_kernel(hid, skp, cot_in, mask_in, *refs, nz):
+    (b0, b1, b2, b3, b4, b5, b6, b7, wm, wt, wo, we, wr,
+     res, hgrad, sgrad, F, WV, G, D,
+     W, X, PR, XH, MID, E, INV, MASK, VEC, DB, MROWS, v0, v1, v2, v3, v4, v5, v6, v7,
+     K, R1, R2, R3, O, VB,
+     loc, loc2, zs, zr, xs, xr, ys, yr, cs, cr, fsem, insem, es, er, dsem, osem,
+     ld, s1, r1, s2, r2, s3, r3, st, sf, rf, sc, rcv, vl, vs, vr) = refs
     dp = lax.axis_index("dp"); z = lax.axis_index("seq")
     c = dp % 2; x = (dp // 2) % 2; y = dp // 4
     xn = dp + 2 - 4 * x; yn = dp + 4 - 8 * y; cn = dp + 1 - 2 * c; co = 1 - c
@@ -128,14 +129,12 @@
     def load_out(j, slot): return pltpu.make_async_copy(slot, G.at[z, j], loc2.at[j])
     for j in range(min(room, NB)): load_in(j).start()
     inputs = [pltpu.make_async_copy(a, b, insem.at[i]) for i, (a, b) in enumerate(
-        ((hid, X.at[HID]), (skp, X.at[SKP]), (cot_in, X.at[COT]), (mask_in, MASK), (vec_in, VEC)))]
+        ((hid.at[0], X.at[HID]), (skp.at[0], X.at[SKP]), (cot_in.at[0], X.at[COT]), (mask_in, MROWS),
+         (b0, v0), (b1, v1), (b2, v2), (b3, v3), (b4, v4), (b5, v5), (b6, v6), (b7, v7)))]
     for cp in inputs: cp.start()
-    for j in range(min(room, NB)):
+    for j in range(4):
         load_in(j).wait()
         load_out(j, stage(j)).start()
-    for j in range(AHEAD + 2): load_out(j, stage(j)).wait()
-    for j in range(room, NB):
-        load_in(j).start()
     pl.semaphore_wait(bar, nz + 2)
 
     half = R // 2; third = half // 3
@@ -147,16 +146,16 @@
     def same(region, ss, rs, dev): return rc(region, region, ss, rs, dev)
     def zcopy(b, d, k):
         s = z - k if d == 0 else z + k
-        return same(reg(s, b, base + third * zp, third), zs.at[b, d, k], zr.at[b, d, k], (dp, z + 1 if d == 0 else z - 1))
+        return same(reg(s, b, base + third * zp, third), zs.at[b % RING, d, k], zr.at[b % RING, d, k], (dp, z + 1 if d == 0 else z - 1))
     def zsend_ok(d, k):
         return (z >= k) & (z < nz - 1) if d == 0 else (z + k <= nz - 1) & (z > 0)
     def zrecv_ok(d, k):
         return z >= k + 1 if d == 0 else z + 1 + k <= nz - 1
     def shard_in(d, k):
         return z - 1 - k if d == 0 else z + 1 + k
-    def xcopy(b, s): return same(reg(s, b, base + third * zp, third), xs.at[b, s], xr.at[b, s], (xn, z))
-    def ycopy(b, s): return same(reg(s, b, base + third * yp, third), ys.at[b, s], yr.at[b, s], (yn, z))
-    def ccopy(b, s): return same(reg(s, b, base, half), cs.at[b, s], cr.at[b, s], (cn, z))
+    def xcopy(b, s): return same(reg(s, b, base + third * zp, third), xs.at[b % 6, s], xr.at[b % 6, s], (xn, z))
+    def ycopy(b, s): return same(reg(s, b, base + third * yp, third), ys.at[b % 6, s], yr.at[b % 6, s], (yn, z))
+    def ccopy(b, s): return same(reg(s, b, base, half), cs.at[b % 6, s], cr.at[b % 6, s], (cn, z))
     def own(b):
         for d in (0, 1):
             @pl.when(zsend_ok(d, 0))
@@ -184,7 +183,9 @@
         ccopy(b, s).wait()
         xcopy(b, s).wait_send()
         ycopy(b, s).wait_send()
-    for j in range(AHEAD): own(j)
+    for j in range(4):
+        load_out(j, stage(j)).wait()
+        if j < AHEAD: own(j)
     def gather_tick(t):
         @pl.when(t < NB - AHEAD)
         def _():
@@ -211,32 +212,32 @@
         return NP - 1 - q // SUB, pl.ds(pl.multiple_of(half * h + T * (q % SUB), 16), T)
     def load(q, s):
         p, rows = piece(q, keep(q, s))
-        return pltpu.make_async_copy(D.at[s, p, rows], K.at[ring(q), s], ld.at[s, q])
+        return pltpu.make_async_copy(D.at[s, p, rows], K.at[ring(q), s], ld.at[s, ring(q)])
     def first(q, s):
         p, rows = piece(q, 1 - keep(q, s))
-        return rc(D.at[s, p, rows], R1.at[ring(q), s], s1.at[s, q], r1.at[s, q], (near(q, s), z))
+        return rc(D.at[s, p, rows], R1.at[ring(q), s], s1.at[s, ring(q)], r1.at[s, ring(q)], (near(q, s), z))
     def up(q, s):
-        return rc(K.at[ring(q), s], R2.at[ring(q), s], s2.at[s, q], r2.at[s, q], (dp, z + 1))
+        return rc(K.at[ring(q), s], R2.at[ring(q), s], s2.at[s, ring(q)], r2.at[s, ring(q)], (dp, z + 1))
     def down(q, s):
         away = jnp.minimum(z - 1 - s, 1)
         slot = nz + away * (s - nz)
-        return rc(K.at[ring(q), s], R2.at[ring(q), slot], s2.at[s, q], r2.at[slot, q], (dp, z - 1))
+        return rc(K.at[ring(q), s], R2.at[ring(q), slot], s2.at[s, ring(q)], r2.at[slot, ring(q)], (dp, z - 1))
     def got(slot, q):
-        return rc(K.at[ring(q), 0], R2.at[ring(q), slot], s2.at[0, q], r2.at[slot, q], (dp, z))
+        return rc(K.at[ring(q), 0], R2.at[ring(q), slot], s2.at[0, ring(q)], r2.at[slot, ring(q)], (dp, z))
     def last(q):
-        return rc(K.at[ring(q), z], R3.at[ring(q)], s3.at[q], r3.at[q], (far(q, z), z))
+        return rc(K.at[ring(q), z], R3.at[ring(q)], s3.at[ring(q)], r3.at[ring(q)], (far(q, z), z))
     def frow(q, h, cc):
         p, rows = piece(q, h)
         return F.at[2 * p + cc, rows]
-    def keepf(q): return pltpu.make_async_copy(O.at[ring(q)], frow(q, keep(q, z), c), st.at[q])
-    def spread(q): return rc(O.at[ring(q)], frow(q, keep(q, z), c), sf.at[q], rf.at[q], (near(q, z), z))
+    def keepf(q): return pltpu.make_async_copy(O.at[ring(q)], frow(q, keep(q, z), c), st.at[ring(q)])
+    def spread(q): return rc(O.at[ring(q)], frow(q, keep(q, z), c), sf.at[ring(q)], rf.at[ring(q)], (near(q, z), z))
     def spread_in(q):
         r = frow(q, 1 - keep(q, z), c)
-        return rc(r, r, sf.at[q], rf.at[q], (near(q, z), z))
-    def cross(q): return rc(O.at[ring(q)], frow(q, keep(q, z), c), sc.at[0, q], rcv.at[0, q], (cn, z))
+        return rc(r, r, sf.at[ring(q)], rf.at[ring(q)], (near(q, z), z))
+    def cross(q): return rc(O.at[ring(q)], frow(q, keep(q, z), c), sc.at[0, ring(q)], rcv.at[0, ring(q)], (cn, z))
     def cross2(q):
         r = frow(q, 1 - keep(q, z), c)
-        return rc(r, r, sc.at[1, q], rcv.at[1, q], (cn, z))
+        return rc(r, r, sc.at[1, ring(q)], rcv.at[1, ring(q)], (cn, z))
     def add(a, b): return (a.astype(f32) + b.astype(f32)).astype(bf16)
     def issue(q):
         for s in range(nz):
@@ -465,11 +466,18 @@
         VB[0] = jnp.zeros_like(VB[0])
         for cp in inputs: cp.wait()
         for n in ("hid", "skp", "cot"): ex[n].start()
-        for j in range(room, NB):
+        valid = MROWS[pl.ds(z, 1), :].astype(f32)
+        MASK[...] = jnp.broadcast_to(valid, (MASK.shape[1], L)).T
+        for i, v in enumerate((v0, v1, v2, v3, v4, v5, v6)):
+            VEC[i:i + 1, :] = v[...].astype(f32).reshape(1, C)
+        for i in range(4):
+            VEC[7 + i:8 + i, :] = v7[C * i:C * (i + 1)].astype(f32).reshape(1, C)
+        for j in range(room, NB): load_in(j).start()
+        for j in range(4, NB):
             load_in(j).wait()
             load_out(j, stage(j)).start()
     def x_stored():
-        for j in range(AHEAD + 2, NB): load_out(j, stage(j)).wait()
+        for j in range(4, NB): load_out(j, stage(j)).wait()
     def x_attended(): ex["att"].start()
     def x_acts():
         arrived("cot")
@@ -477,7 +485,7 @@
     def x_result():
         ex["px0"].start(); ex["px1"].start()
         X[OUT] = (MID[...] + E[0] + vec(6)).astype(bf16)
-        pltpu.make_async_copy(X.at[OUT], res, osem.at[0]).start()
+        pltpu.make_async_copy(X.at[OUT], res.at[0], osem.at[0]).start()
         up_ = X[COT].astype(f32)
         MID[...] = up_
         tally(6, up_)
@@ -489,9 +497,9 @@
         ex["qk"].wait_send(); qk_in().wait_recv()
     def x_merge(): arrived("hid", "skp", "gr")
     def x_outs():
-        pltpu.make_async_copy(X.at[OUT], res, osem.at[0]).wait()
+        pltpu.make_async_copy(X.at[OUT], res.at[0], osem.at[0]).wait()
     def x_last():
-        outs = [pltpu.make_async_copy(X.at[OUT + i], (hgrad, sgrad)[i], osem.at[1 + i]) for i in range(2)]
+        outs = [pltpu.make_async_copy(X.at[OUT + i], (hgrad, sgrad)[i].at[0], osem.at[1 + i]) for i in range(2)]
         for cp in outs: cp.start()
         for cp in outs: cp.wait()
     extras = [x_begin, x_stored, x_attended, x_acts, x_result, x_px, x_triple, x_heads, x_merge, x_outs, x_last,
@@ -527,54 +535,79 @@
 
 
 def block(hidden, skipped, cotangent, mask, vectors, weights, nz):
-    L, C = hidden.shape
+    L, C = hidden.shape[1:]
     R = weights[2].shape[0]
     T = R // 2 // SUB
     S = pltpu.SemaphoreType.DMA
     V = pltpu.VMEM
-    rows = jax.ShapeDtypeStruct((L, C), bf16)
+    rows = jax.ShapeDtypeStruct((1, L, C), bf16)
     hbm = pl.BlockSpec(memory_space=pl.ANY)
     out_shape = (rows, rows, rows, jax.ShapeDtypeStruct((NB, R, C), bf16), jax.ShapeDtypeStruct((VR, C), f32),
                  jax.ShapeDtypeStruct((nz, NB, R, C), bf16), jax.ShapeDtypeStruct((nz, NP, R, C), bf16))
     scratch = [
         V((SLOTS, 4, R, C), bf16), V((PLACES, L, C), bf16), V((HEADS, L, L), bf16), V((2, L, C), f32), V((L, C), f32),
         V((2, L, C), f32), V((2, L, 128), f32), V((L, 128), f32), V((VR, C), f32), V((4 * R, C), bf16),
+        V(mask.shape, jnp.int32), *[V(v.shape, bf16) for v in vectors],
         V((RING, nz, T, C), bf16), V((RING, nz, T, C), bf16), V((RING, nz + 1, T, C), bf16), V((RING, T, C), bf16), V((RING, T, C), bf16),
         V((6 + nz, VR, C), f32),
-        S((NB,)), S((NB,)), S((NB, 2, nz - 1)), S((NB, 2, nz - 1)), S((NB, nz)), S((NB, nz)), S((NB, nz)), S((NB, nz)), S((NB, nz)), S((NB, nz)),
-        S((SLOTS, 4)), S((5,)), S((16,)), S((16,)), S((4,)), S((3,)),
-        S((nz, Q)), S((nz, Q)), S((nz, Q)), S((nz, Q)), S((nz + 1, Q)), S((Q,)), S((Q,)), S((Q,)), S((Q,)), S((Q,)), S((2, Q)), S((2, Q)),
+        S((NB,)), S((NB,)), S((RING, 2, nz - 1)), S((RING, 2, nz - 1)), S((6, nz)), S((6, nz)), S((6, nz)), S((6, nz)), S((6, nz)), S((6, nz)),
+        S((SLOTS, 4)), S((12,)), S((16,)), S((16,)), S((4,)), S((3,)),
+        S((nz, RING)), S((nz, RING)), S((nz, RING)), S((nz, RING)), S((nz + 1, RING)), S((RING,)), S((RING,)), S((RING,)), S((RING,)), S((RING,)), S((2, RING)), S((2, RING)),
         S((2,)), S((2 + nz,)), S((2 + nz,)),
     ]
     return pl.pallas_call(
         functools.partial(block_kernel, nz=nz),
-        out_shape=out_shape, in_specs=[hbm] * 10, out_specs=(hbm,) * 7, scratch_shapes=scratch,
+        out_shape=out_shape, in_specs=[hbm] * 17, out_specs=(hbm,) * 7, scratch_shapes=scratch,
         compiler_params=pltpu.CompilerParams(collective_id=0, has_side_effects=True, vmem_limit_bytes=63 * 2**20),
-    )(hidden, skipped, cotangent, mask, vectors, *weights)[:5]
-
-
-def unpack_kernel(F, m, t, o, e, r):
-    i = pl.program_id(0)
-    for out, lo, n in ((m, 0, 2), (t, 2, 3), (o, 5, 1), (e, 6, 4), (r, 10, 4)):
-        @pl.when((i >= lo) & (i < lo + n))
-        def _(): out[...] = F[0].astype(f32)
-
-
-def unpack(F):
+    )(hidden, skipped, cotangent, mask, *vectors, *weights)[:5]
+
+
+def unpack_kernel(F, WV, i0, i1, i2, m, t, o, e, r, o0, o1, o2, *rest):
+    vec_outs, (FB, OB, VB, IB), vbufs, (fin, fout, vin, vout, iin, iout) = rest[:8], rest[8:12], rest[12:20], rest[20:]
+    R, C = FB.shape[1:]
+    outs = block_slices((m, t, o, e, r))
+    takes = [pltpu.make_async_copy(F.at[j], FB.at[j], fin.at[j]) for j in range(NB)]
+    puts = [pltpu.make_async_copy(OB.at[j], outs[j], fout.at[j]) for j in range(NB)]
+    sums = pltpu.make_async_copy(WV, VB, vin.at[0])
+    images = [(pltpu.make_async_copy(a, IB.at[i], iin.at[i]), pltpu.make_async_copy(IB.at[i], b, iout.at[i]))
+              for i, (a, b) in enumerate(((i0, o0), (i1, o1), (i2, o2)))]
+    for cp in takes[:4]: cp.start()
+    sums.start()
+    for a, _ in images: a.start()
+    for cp in takes[4:]: cp.start()
+    for j in range(NB):
+        takes[j].wait()
+        OB[j] = FB[j].astype(f32)
+        puts[j].start()
+        if j == 3:
+            sums.wait()
+            for i in range(7): vbufs[i][...] = VB[i:i + 1, :].reshape(C)
+            for i in range(4): vbufs[7][C * i:C * (i + 1)] = VB[7 + i:8 + i, :].reshape(C)
+            small = [pltpu.make_async_copy(a, b, vout.at[i]) for i, (a, b) in enumerate(zip(vbufs, vec_outs))]
+            for cp in small: cp.start()
+            for a, b in images:
+                a.wait()
+                b.start()
+    for cp in puts: cp.wait()
+    for cp in small: cp.wait()
+    for _, b in images: b.wait()
+
+
+def unpack(images, F, sums):
     R, C = F.shape[1:]
-    def spot(lo, n, along):
-        def index(i):
-            j = jnp.clip(i - lo, 0, n - 1)
-            return (j, 0) if along == 0 else (0, j)
-        return pl.BlockSpec((R, C), index)
-    shapes = [(2 * R, C), (R, 3 * C), (R, C), (R, 4 * C), (4 * R, C)]
+    S = pltpu.SemaphoreType.DMA
+    hbm = pl.BlockSpec(memory_space=pl.ANY)
+    vecs = [jax.ShapeDtypeStruct((n * C,), f32) for n in (1, 1, 1, 1, 1, 1, 1, 4)]
+    shapes = [jax.ShapeDtypeStruct(s, f32) for s in ((2 * R, C), (R, 3 * C), (R, C), (R, 4 * C), (4 * R, C))]
+    shapes += [jax.ShapeDtypeStruct(a.shape, a.dtype) for a in images] + vecs
     return pl.pallas_call(
-        unpack_kernel, grid=(NB,),
-        out_shape=[jax.ShapeDtypeStruct(s, f32) for s in shapes],
-        in_specs=[pl.BlockSpec((1, R, C), lambda i: (i, 0, 0))],
-        out_specs=[spot(0, 2, 0), spot(2, 3, 1), spot(5, 1, 0), spot(6, 4, 1), spot(10, 4, 0)],
-        compiler_params=pltpu.CompilerParams(vmem_limit_bytes=48 * 2**20),
-    )(F)
+        unpack_kernel, out_shape=shapes, in_specs=[hbm] * 5, out_specs=[hbm] * len(shapes),
+        scratch_shapes=[pltpu.VMEM((NB, R, C), bf16), pltpu.VMEM((NB, R, C), f32), pltpu.VMEM(sums.shape, f32),
+                        pltpu.VMEM((3,) + images[0].shape, bf16), *[pltpu.VMEM(v.shape, f32) for v in vecs],
+                        S((NB,)), S((NB,)), S((1,)), S((8,)), S((3,)), S((3,))],
+        compiler_params=pltpu.CompilerParams(vmem_limit_bytes=63 * 2**20),
+    )(F, sums, *images)
+
 
 def pack(m, t, o, e, r):
     R, C = o.shape
@@ -704,16 +737,12 @@
 
 def body(hidden, skipped, row_mask, cotangent, merge_weight, merge_bias, first_gain, first_shift, triple_weight,
          output_weight, output_bias, second_gain, second_shift, expand_weight, expand_bias, reduce_weight, reduce_bias):
-    L, C = hidden.shape[1:]
-    nz = lax.axis_size("seq")
-    valid = lax.dynamic_index_in_dim(row_mask, lax.axis_index("seq"), 0, False)
-    mask = jnp.broadcast_to(valid.astype(f32)[:, None], (L, 128))
-    vectors = jnp.concatenate([
-        merge_bias, first_gain, first_shift, output_bias, second_gain, second_shift, reduce_bias, expand_bias,
-        jnp.zeros(((VR - 11) * C,), bf16)]).astype(f32).reshape(VR, C)
+    vectors = (merge_bias, first_gain, first_shift, output_bias, second_gain, second_shift, reduce_bias, expand_bias)
     weights = (merge_weight, triple_weight, output_weight, expand_weight, reduce_weight)
-    *images, F, sums = block(hidden[0], skipped[0], cotangent[0], mask, vectors, weights, nz)
-    return outputs(images, unpack(F), sums)
+    *images, F, sums = block(hidden, skipped, cotangent, row_mask, vectors, weights, lax.axis_size("seq"))
+    merge, triple, output, expand, reduce, result, hidden_grad, skipped_grad, *v = unpack(images, F, sums)
+    return (result, hidden_grad, skipped_grad, merge, v[0], v[1], v[2], triple, output, v[3], v[4], v[5], expand, v[7],
+            reduce, v[6])
 
 
 def solution(mesh):

time: 370 us -> 341 us (0.922)
  Pallas kernels: 353 us -> 338 us
  local copies, waits for them, and re-layouts: 14.7 us -> 0 us
    pallas_call x1, Pallas kernels: 338 us -> 327 us  [block(): pl.pallas_call(functools.partial(block_kernel, nz=nz), out_shape=out_shap...]
    unnamed x17 -> x0, local copies, waits for them, and re-layouts: 9.57 us -> none
where the time goes in v2:
time: 341 us; the launch traced here: 339 us
  Pallas kernels  338 us (99%)
    pallas_call x1, Pallas kernels, block(): pl.pallas_call(functools.partial(block_kernel, nz=nz), out_shape=out_shap...  327 us
    pallas_call x1, Pallas kernels, unpack(): pl.pallas_call(unpack_kernel, out_shape=shapes, in_specs=[hbm] * 5, out_s...  11.5 us

profile of v2, /device:TPU:0, one launch (start us, length us, event | category | flops | bytes accessed | tf_op | source)
XLA Modules:
  0.0 339.0 jit_solution(422334024791397829)
XLA Ops:
  0.7 326.7 %shard_map.288 = (bf16[1,272,1152]{2,1,0:T(8,128)(2,1)}, bf16[1,272,1152]{2,1,0:T(8,128)(2,1)}, bf16[1,272,1152]{2,1,0:T(8,128)(2,1)}, bf16[14,288,1152]{2,1,0:T...) custom-call(bf16[1,272,1152]{2,1,0:T(8,128)(2,1)} %hid.1, ...), custom_call_target="tpu_custom_call" | custom-call | tf_op jit(solution)/shard_map/pallas_call | solution.py:558
  327.3 11.5 %shard_map.289 = (f32[576,1152]{1,0:T(8,128)}, f32[288,3456]{1,0:T(8,128)}, f32[288,1152]{1,0:T(8,128)}, f32[288,4608]{1,0:T(8,128)}, f32[1152,1152]{1,0:T(8,128...) custom-call(bf16[14,288,1152]{2,1,0:T(8,128)(2,1)} %get-tuple-elemen, ...), custom_call_target="tpu_custom_call" | custom-call | tf_op jit(solution)/shard_map/pallas_call | solution.py:603

commit v3 on v2

--- a/solution.py
+++ b/solution.py
@@ -19,7 +19,7 @@
 SLOTS = 3
 VR = 16
 READY = 5
-LEAD = READY + 10
+LEAD = READY + 11
 f32, bf16 = jnp.float32, jnp.bfloat16
 
 
@@ -47,49 +47,61 @@
     return lax.dot_general(a, b, (((0,), (0,)), ((), ())), preferred_element_type=f32)
 
 
-HID, SKP, COT, NORMED, ATT, TWO, ACT, TRI, BR, TG, GR, EXP, PX, ATTG, OUT, PLACES = 0, 2, 4, 6, 8, 10, 12, 20, 23, 25, 31, 33, 37, 39, 40, 42
+HID, SKP, COT, NORMED, ATT, TWO, ACT, TRI, BR, TG, GR, EXP, ATTG, PLACES = 0, 2, 4, 6, 8, 10, 12, 20, 23, 25, 31, 33, 41, 42
+HGRAD, SGRAD, RESULT = NORMED, TWO, ATT
 NN, NT, EXTRA, CAST, FETCH, NORM, NORM_BACK, GELU, GELU_BACK, ATTEND, ATTEND_BACK, ROWS, FULL = range(1, 14)
 
 
-def op(mode, a=0, w=0, acc=0, e=0, wait=1, pre=None, post=None):
+def op(mode, a=0, w=0, acc=0, wait=1, pre=None, post=None):
     pre, post = (0 if v is None else v + 1 for v in (pre, post))
-    return mode + 16 * (a + 64 * (w + 32 * (acc + 2 * (e + 2 * (wait + 2 * (pre + 32 * post))))))
+    return mode + 16 * (a + 64 * (w + 32 * (acc + 2 * (wait + 2 * (pre + 32 * post)))))
 
 
 def plan():
     B = READY
-    ops = [(0, op(EXTRA, 0)), (1, op(EXTRA, 1))]
-    ops += [(B + 1, o) for o in (op(FETCH, 0), op(NN, HID, 0, pre=1), op(NN, SKP, 1, acc=1), op(NORM, 0))]
+    ops = []
+    def at(tick, *what): ops.extend((tick, o) for o in what)
+    (begin, stored, cot, attended, acts, pairs, px, triple, heads, merge, joined, result, outs, *sums) = (op(EXTRA, i) for i in range(18))
+    at(0, begin)
+    at(1, stored)
+    at(2, cot)
+    at(B + 1, op(FETCH, 0), op(NN, HID, 0, pre=1), op(NN, SKP, 1, acc=1), op(NORM, 0))
     for j in range(3):
-        ops += [(B + 2 + j, o) for o in (op(NN, NORMED, 2 + j, pre=2 + j), op(CAST, TRI + j))]
-    ops += [(B + 4, op(ATTEND, 0)), (B + 4, op(ATTEND, 1)), (B + 5, op(ATTEND, 2)), (B + 5, op(ATTEND, 3)), (B + 5, op(EXTRA, 2))]
-    ops += [(B + 5, op(NN, ATT, 5, pre=5)), (B + 5, op(NORM, 1))]
+        at(B + 2 + j, op(NN, NORMED, 2 + j, pre=2 + j), op(CAST, TRI + j))
+    at(B + 4, op(ATTEND, 0), op(ATTEND, 1))
+    at(B + 5, op(ATTEND, 2), op(ATTEND, 3), attended, op(NN, ATT, 5, pre=5), op(NORM, 1))
     for i in range(4):
-        ops += [(B + 6 + i, op(NN, TWO, 6 + i, pre=6 + i)), (B + 6 + i, op(GELU, i))]
-    ops += [(B + 9, op(EXTRA, 3)), (B + 9, op(ROWS, 0)), (B + 10, op(ROWS, 1))]
-    ops += [(B + 13, op(FETCH, 10 + i)) for i in range(3)]
+        at(B + 6 + i, op(NN, TWO, 6 + i, pre=6 + i), op(GELU, i))
+    at(B + 9, acts, op(ROWS, 0))
+    at(B + 11, op(ROWS, 1))
+    at(B + 13, op(FETCH, 10), op(FETCH, 11), op(FETCH, 12))
     for i in range(4):
-        ops += [(B + 13 + i // 2, o) for o in (
-            op(NN, ACT + 2 * i, 10 + i, acc=int(i > 0)), op(NT, COT, 10 + i, e=1, wait=0, post=13 + i), op(GELU_BACK, i))]
-    ops += [(B + 14, op(EXTRA, 4)), (B + 15, op(EXTRA, 5)), (B + 15, op(FULL, 0)), (B + 16, op(FULL, 1))]
+        at(B + 13 + i // 2, op(NT, COT, 10 + i, post=13 + i), op(GELU_BACK, i))
+    at(B + 14, pairs)
+    at(B + 15, px, op(FULL, 0))
     for i in range(4):
-        ops += [(B + 16 + (i > 0), op(NT, EXP + i, 14 + i, acc=int(i > 0), post=17 + i))]
-    ops += [(B + 17, op(NORM_BACK, 1)), (B + 18, op(NT, BR, 18, post=21)), (B + 18, op(CAST, ATTG))]
-    ops += [(B + 18 + g // 2, op(ATTEND_BACK, g)) for g in range(4)]
-    ops += [(B + 19, op(EXTRA, 6)), (B + 20, op(EXTRA, 7)), (B + 20, op(FULL, 2)), (B + 21, op(FULL, 3))]
-    for j in range(3):
-        ops += [(B + 22, op(NT, TG + 2 * j, 19 + j, acc=int(j > 0), post=22 + j if j < 2 else None))]
-    ops += [(B + 23, op(NORM_BACK, 0)), (B + 24, op(EXTRA, 8)), (B + 24, op(ROWS, 2)), (B + 25, op(EXTRA, 9))]
-    for i in range(2):
-        ops += [(B + 25, op(NT, GR, 22 + i)), (B + 25, op(CAST, OUT + i))]
-    ops += [(B + 25, op(EXTRA, 10))]
-    ops += [(B + t, op(EXTRA, 11 + i)) for i, t in enumerate((26, 27, 28, 29, 32))]
+        at(B + 16 + i // 2, op(NT, EXP + 2 * i, 14 + i, acc=int(i > 0), post=17 + i))
+    at(B + 17, op(NORM_BACK, 1))
+    at(B + 18, op(NT, BR, 18, post=21), op(CAST, ATTG), op(FULL, 1))
+    at(B + 19, op(ATTEND_BACK, 0), op(ATTEND_BACK, 1))
+    at(B + 20, op(ATTEND_BACK, 2), op(ATTEND_BACK, 3), triple)
+    at(B + 21, heads, op(FULL, 2))
+    at(B + 22, op(NT, TG, 19, post=22), op(NT, TG + 2, 20, acc=1, post=23))
+    at(B + 23, op(NT, TG + 4, 21, acc=1, post=24), op(NORM_BACK, 0))
+    at(B + 24, op(FULL, 3))
+    at(B + 26, merge, op(ROWS, 2))
+    at(B + 26, sums[0], op(NT, GR, 22, post=25), op(CAST, HGRAD))
+    at(B + 27, sums[1], op(NT, GR, 23, post=26), op(CAST, SGRAD), joined)
+    at(B + 28, sums[2], op(NN, ACT, 24, post=27), op(NN, ACT + 2, 25, acc=1))
+    at(B + 29, sums[3], op(NN, ACT + 4, 26, acc=1), op(NN, ACT + 6, 27, acc=1), result)
+    at(B + 30, outs)
+    at(B + 32, sums[4])
     return ops
 
 
 OPS = plan()
 STARTS = [sum(t < tick for t, _ in OPS) for tick in range(LEAD + AHEAD + Q + 10)]
-UNITS = [2, 6] + [4 * j for j in range(2, 10)] + [1 + 4 * s for s in range(4)] + [4 * j for j in (6, 7, 8, 9, 5, 2, 3, 4)] + [2, 6]
+UNITS = [2, 6] + [4 * j for j in range(2, 10)] + [1 + 4 * s for s in range(4)] + [4 * j for j in (6, 7, 8, 9, 5, 2, 3, 4)] + [2, 6] + [1 + 4 * s for s in range(4)]
 
 
 def lookup(values, i):
@@ -103,7 +115,7 @@
 def block_kernel(hid, skp, cot_in, mask_in, *refs, nz):
     (b0, b1, b2, b3, b4, b5, b6, b7, wm, wt, wo, we, wr,
      res, hgrad, sgrad, F, WV, G, D,
-     W, X, PR, XH, MID, E, INV, MASK, VEC, DB, MROWS, v0, v1, v2, v3, v4, v5, v6, v7,
+     W, X, PR, XH, MID, MG, E, INV, MASK, VEC, DB, MROWS, v0, v1, v2, v3, v4, v5, v6, v7,
      K, R1, R2, R3, O, VB,
      loc, loc2, zs, zr, xs, xr, ys, yr, cs, cr, fsem, insem, es, er, dsem, osem,
      ld, s1, r1, s2, r2, s3, r3, st, sf, rf, sc, rcv, vl, vs, vr) = refs
@@ -246,12 +258,13 @@
         for s in range(nz):
             load(q, s).wait(); first(q, s).wait_recv()
             K[ring(q), s] = add(K[ring(q), s], R1[ring(q), s])
-            if s > 0:
-                @pl.when(z == 0)
-                def _(): up(q, s).start()
+        for s in range(nz):
             if s < nz - 1:
                 @pl.when(z == nz - 1)
                 def _(): down(q, s).start()
+            if nz - 1 - s > 0:
+                @pl.when(z == 0)
+                def _(): up(q, nz - 1 - s).start()
     def hop(q, k):
         for s in range(nz):
             if s > k:
@@ -298,12 +311,15 @@
     steps = [(0, start)] + [(k, functools.partial(hop, k=k)) for k in range(1, nz - 1)] + [
         (nz - 1, arrive), (nz, final), (nz + 1, relay), (nz + 3, drain)]
     def sum_tick(t):
-        @pl.when((t >= 0) & (t < Q))
-        def _(): issue(t)
         for off, fn in steps:
             q = t - AHEAD - off
             @pl.when((q >= 0) & (q < Q))
             def _(): fn(q)
+        @pl.when((t % SUB == 0) & (t < Q))
+        def _():
+            for cp in puts(NP - 1 - t // SUB): cp.wait()
+        @pl.when(t < Q)
+        def _(): issue(t)
 
     devs = ((cn, z), (xn, z), (yn, z))
     def swap(i): return rc(VB.at[2 * i], VB.at[2 * i + 1], vs.at[i], vr.at[i], devs[i])
@@ -331,10 +347,10 @@
     def both(i, a): return pair(i, X.at[a], X.at[a + 1])
     ex = {
         "hid": both(0, HID), "skp": both(1, SKP), "cot": both(2, COT), "normed": both(3, NORMED), "att": both(4, ATT), "two": both(5, TWO),
-        "px0": pair(10, X.at[EXP + co], X.at[PX]), "px1": pair(11, X.at[EXP + co + 2], X.at[PX + 1]), "br": both(12, BR),
+        "px0": both(10, EXP + 2 * co), "px1": both(11, EXP + 2 * co + 4), "br": both(12, BR),
         "qk": both(13, TG + 2 * co), "v": both(14, TG + 4), "gr": both(15, GR),
     }
-    def qk_in(): return both(13, TG + 2 * c)
+    def arrives(i, a): return both(i, a).wait_recv()
     def send_act(i): return both(6 + i, ACT + 2 * i)
     def arrived(*names):
         for n in names: ex[n].wait()
@@ -353,19 +369,19 @@
     def vec(i): return VEC[pl.ds(i, 1), :]
     def tally(i, v): VB[0, pl.ds(i, 1), :] = jnp.sum(v, axis=0, keepdims=True)
 
-    def do_matmul(dot, a, n, acc, e, wait, pre, post):
+    def do_matmul(dot, a, n, acc, wait, pre, post):
         @pl.when(pre > 0)
         def _(): fetch(pre - 1)
         @pl.when(wait > 0)
         def _(): fetched(n)
         v = dot(X[a], weight(n))
-        E[e] = jnp.where(acc > 0, E[e], 0.0) + v
+        E[...] = jnp.where(acc > 0, E[...], 0.0) + v
         @pl.when(post > 0)
         def _(): fetch(post - 1)
     def do_cast(a):
-        X[a] = E[0].astype(bf16)
+        X[a] = E[...].astype(bf16)
     def do_norm(k):
-        v = jnp.where(k > 0, MID[...], 0.0) + E[0] + vec(3 * k)
+        v = jnp.where(k > 0, MID[...], 0.0) + E[...] + vec(3 * k)
         MID[...] = v
         m = v - jnp.mean(v, axis=-1, keepdims=True)
         r = lax.rsqrt(jnp.mean(m * m, axis=-1, keepdims=True) + EPS)
@@ -375,14 +391,14 @@
         X[a] = (m * r * vec(3 * k + 1) + vec(3 * k + 2)).astype(bf16)
         both(3 + 2 * k, a).start()
     def do_norm_back(k):
-        e = E[0]
+        e = E[...]
         xhat = XH[k]
         tally(3 * k + 1, e * xhat); tally(3 * k + 2, e)
         t = e * vec(3 * k + 1)
         a = jnp.mean(t, axis=-1, keepdims=True)
         b = jnp.mean(t * xhat, axis=-1, keepdims=True)
-        v = MID[...] + (t - a - xhat * b) * INV[k, :, 0:1]
-        MID[...] = v
+        v = jnp.where(k > 0, X[COT].astype(f32), MG[...]) + (t - a - xhat * b) * INV[k, :, 0:1]
+        MG[...] = v
         low = v.astype(bf16)
         a = GR + (BR - GR) * k
         X[a] = low
@@ -392,17 +408,17 @@
     def part(n): return pl.ds(pl.multiple_of(step * n, 128), step)
     def do_gelu(i):
         def one(n, _):
-            v = E[0, :, part(n)] + VEC[pl.ds(7 + i, 1), part(n)]
+            v = E[:, part(n)] + VEC[pl.ds(7 + i, 1), part(n)]
             cdf = 0.5 * (1.0 + lax.erf(v * (0.5 ** 0.5)))
             X[ACT + 2 * i, :, part(n)] = (v * cdf).astype(bf16)
-            X[EXP + i, :, part(n)] = (cdf + v * jnp.exp(-0.5 * v * v) * 0.3989422804014327).astype(bf16)
+            X[EXP + 2 * i, :, part(n)] = (cdf + v * jnp.exp(-0.5 * v * v) * 0.3989422804014327).astype(bf16)
             return 0
         lax.fori_loop(0, 3, one, 0)
         send_act(i).start()
     def do_gelu_back(i):
         def one(n, _):
-            low = (E[1, :, part(n)] * X[EXP + i, :, part(n)].astype(f32)).astype(bf16)
-            X[EXP + i, :, part(n)] = low
+            low = (E[:, part(n)] * X[EXP + 2 * i, :, part(n)].astype(f32)).astype(bf16)
+            X[EXP + 2 * i, :, part(n)] = low
             VB[0, pl.ds(7 + i, 1), part(n)] = jnp.sum(low.astype(f32), axis=0, keepdims=True)
             return 0
         lax.fori_loop(0, 3, one, 0)
@@ -433,10 +449,10 @@
                     sg = (pf * (pg - jnp.sum(pf * pg, axis=0, keepdims=True))).astype(bf16)
                     X[TG, :, sl] = (tn(sg, k) * scale).astype(bf16)
                     X[TG + 2, :, sl] = (nn(sg, q) * scale).astype(bf16)
+    def puts(p): return [pltpu.make_async_copy(DB.at[pl.ds(R * s, R)], D.at[s, p], dsem.at[s]) for s in range(4)]
     def put(p):
-        cps = [pltpu.make_async_copy(DB.at[pl.ds(R * s, R)], D.at[s, p], dsem.at[s]) for s in range(4)]
-        for cp in cps: cp.start()
-        for cp in cps: cp.wait()
+        for cp in puts(p): cp.start()
+    def pair_of(a, cols=slice(None)): return X[pl.ds(a, 2), :, cols].reshape(2 * L, -1)
     def do_rows(kind):
         merge = kind // 2
         right = COT + (GR - COT) * merge
@@ -447,17 +463,15 @@
             for v in range(4):
                 @pl.when(cut == v)
                 def _():
-                    sl = slice(R * v, R * v + R)
-                    DB[rows] = (tn(X[left, :, sl], X[right]) + tn(X[left + 1, :, sl], X[right + 1])).astype(bf16)
+                    DB[rows] = tn(pair_of(left, slice(R * v, R * v + R)), pair_of(right)).astype(bf16)
             return 0
         lax.fori_loop(0, 4, one, 0)
         put(6 - kind - 4 * merge)
     def do_full(kind):
         left = jnp.where(kind < 2, TWO, jnp.where(kind == 2, NORMED + (ATT - NORMED) * c, NORMED))
-        right = jnp.where(kind == 0, EXP + 2 + c, jnp.where(kind == 1, EXP + c, jnp.where(kind == 2, TG + 4 + (BR - TG - 4) * c, TG + 2 * c)))
-        other = jnp.where(kind == 0, PX + 1, jnp.where(kind == 1, PX, right + 1))
+        right = jnp.where(kind < 2, EXP + 2 * c + 4 * (1 - kind), jnp.where(kind == 2, TG + 4 + (BR - TG - 4) * c, TG + 2 * c))
         def one(n, _):
-            DB[pl.ds(pl.multiple_of(step * n, 128), step)] = (tn(X[left, :, part(n)], X[right]) + tn(X[left + 1, :, part(n)], X[other])).astype(bf16)
+            DB[pl.ds(pl.multiple_of(step * n, 128), step)] = tn(pair_of(left, part(n)), pair_of(right)).astype(bf16)
             return 0
         lax.fori_loop(0, 3, one, 0)
         put(4 - kind)
@@ -482,27 +496,29 @@
     def x_acts():
         arrived("cot")
         for i in range(4): send_act(i).wait()
+    def x_cot(): tally(6, X[COT].astype(f32))
+    def x_pairs():
+        ex["px0"].start(); ex["px1"].start()
+    def out(i):
+        return pltpu.make_async_copy(X.at[(RESULT, HGRAD, SGRAD)[i]], (res, hgrad, sgrad)[i].at[0], osem.at[i])
     def x_result():
-        ex["px0"].start(); ex["px1"].start()
-        X[OUT] = (MID[...] + E[0] + vec(6)).astype(bf16)
-        pltpu.make_async_copy(X.at[OUT], res.at[0], osem.at[0]).start()
-        up_ = X[COT].astype(f32)
-        MID[...] = up_
-        tally(6, up_)
-    def x_px(): arrived("px0", "px1", "two")
+        X[RESULT] = (MID[...] + E[...] + vec(6)).astype(bf16)
+        out(0).start()
+    def x_joined():
+        out(1).start(); out(2).start()
+    def x_outs():
+        for i in range(3): out(i).wait()
+    def x_px():
+        arrived("two")
+        for i in range(2):
+            ex["px" + str(i)].wait_send(); arrives(10 + i, EXP + 2 * c + 4 * i)
     def x_triple():
         ex["qk"].start(); ex["v"].start()
     def x_heads():
         arrived("normed", "att", "br", "v")
-        ex["qk"].wait_send(); qk_in().wait_recv()
+        ex["qk"].wait_send(); arrives(13, TG + 2 * c)
     def x_merge(): arrived("hid", "skp", "gr")
-    def x_outs():
-        pltpu.make_async_copy(X.at[OUT], res.at[0], osem.at[0]).wait()
-    def x_last():
-        outs = [pltpu.make_async_copy(X.at[OUT + i], (hgrad, sgrad)[i].at[0], osem.at[1 + i]) for i in range(2)]
-        for cp in outs: cp.start()
-        for cp in outs: cp.wait()
-    extras = [x_begin, x_stored, x_attended, x_acts, x_result, x_px, x_triple, x_heads, x_merge, x_outs, x_last,
+    extras = [x_begin, x_stored, x_cot, x_attended, x_acts, x_pairs, x_px, x_triple, x_heads, x_merge, x_joined, x_result, x_outs,
               functools.partial(vstep, 0), functools.partial(vstep, 1), functools.partial(vstep, 2), vline, vend]
     def do_extra(i):
         for k, fn in enumerate(extras):
@@ -512,13 +528,13 @@
     def run(n, _):
         code = lookup([op for _, op in OPS], n)
         mode, a, w = code % 16, code // 16 % 64, code // 1024 % 32
-        acc, e, wait = code // 2 ** 15 % 2, code // 2 ** 16 % 2, code // 2 ** 17 % 2
-        pre, post = code // 2 ** 18 % 32, code // 2 ** 23 % 32
+        acc, wait = code // 2 ** 15 % 2, code // 2 ** 16 % 2
+        pre, post = code // 2 ** 17 % 32, code // 2 ** 22 % 32
         small = ((do_extra, EXTRA), (do_cast, CAST), (fetch, FETCH), (do_norm, NORM), (do_norm_back, NORM_BACK), (do_gelu, GELU),
                  (do_gelu_back, GELU_BACK), (do_attend, ATTEND), (do_attend_back, ATTEND_BACK), (do_rows, ROWS), (do_full, FULL))
         for dot, m in ((nn, NN), (nt, NT)):
             @pl.when(mode == m)
-            def _(): do_matmul(dot, a, w, acc, e, wait, pre, post)
+            def _(): do_matmul(dot, a, w, acc, wait, pre, post)
         for fn, m in small:
             @pl.when(mode == m)
             def _(): fn(a)
@@ -545,8 +561,8 @@
     out_shape = (rows, rows, rows, jax.ShapeDtypeStruct((NB, R, C), bf16), jax.ShapeDtypeStruct((VR, C), f32),
                  jax.ShapeDtypeStruct((nz, NB, R, C), bf16), jax.ShapeDtypeStruct((nz, NP, R, C), bf16))
     scratch = [
-        V((SLOTS, 4, R, C), bf16), V((PLACES, L, C), bf16), V((HEADS, L, L), bf16), V((2, L, C), f32), V((L, C), f32),
-        V((2, L, C), f32), V((2, L, 128), f32), V((L, 128), f32), V((VR, C), f32), V((4 * R, C), bf16),
+        V((SLOTS, 4, R, C), bf16), V((PLACES, L, C), bf16), V((HEADS, L, L), bf16), V((2, L, C), f32), V((L, C), f32), V((L, C), f32),
+        V((L, C), f32), V((2, L, 128), f32), V((L, 128), f32), V((VR, C), f32), V((4 * R, C), bf16),
         V(mask.shape, jnp.int32), *[V(v.shape, bf16) for v in vectors],
         V((RING, nz, T, C), bf16), V((RING, nz, T, C), bf16), V((RING, nz + 1, T, C), bf16), V((RING, T, C), bf16), V((RING, T, C), bf16),
         V((6 + nz, VR, C), f32),

time: 341 us -> 325 us (0.953)
  Pallas kernels: 338 us -> 323 us
    pallas_call x1, Pallas kernels: 327 us -> 312 us  [block(): pl.pallas_call(functools.partial(block_kernel, nz=nz), out_shape=out_shap...]
where the time goes in v3:
time: 325 us; the launch traced here: 324 us
  Pallas kernels  323 us (99%)
    pallas_call x1, Pallas kernels, block(): pl.pallas_call(functools.partial(block_kernel, nz=nz), out_shape=out_shap...  312 us
    pallas_call x1, Pallas kernels, unpack(): pl.pallas_call(unpack_kernel, out_shape=shapes, in_specs=[hbm] * 5, out_s...  11.5 us

profile of v3, /device:TPU:0, one launch (start us, length us, event | category | flops | bytes accessed | tf_op | source)
XLA Modules:
  0.0 324.2 jit_solution(2306518280848550548)
XLA Ops:
  0.7 311.9 %shard_map.288 = (bf16[1,272,1152]{2,1,0:T(8,128)(2,1)}, bf16[1,272,1152]{2,1,0:T(8,128)(2,1)}, bf16[1,272,1152]{2,1,0:T(8,128)(2,1)}, bf16[14,288,1152]{2,1,0:T...) custom-call(bf16[1,272,1152]{2,1,0:T(8,128)(2,1)} %hid.1, ...), custom_call_target="tpu_custom_call" | custom-call | tf_op jit(solution)/shard_map/pallas_call | solution.py:574
  312.5 11.5 %shard_map.289 = (f32[576,1152]{1,0:T(8,128)}, f32[288,3456]{1,0:T(8,128)}, f32[288,1152]{1,0:T(8,128)}, f32[288,4608]{1,0:T(8,128)}, f32[1152,1152]{1,0:T(8,128...) custom-call(bf16[14,288,1152]{2,1,0:T(8,128)(2,1)} %get-tuple-elemen, ...), custom_call_target="tpu_custom_call" | custom-call | tf_op jit(solution)/shard_map/pallas_call | solution.py:619

commit v4 on v3

--- a/solution.py
+++ b/solution.py
@@ -19,7 +19,7 @@
 SLOTS = 3
 VR = 16
 READY = 5
-LEAD = READY + 11
+LEAD = READY + 9
 f32, bf16 = jnp.float32, jnp.bfloat16
 
 
@@ -68,39 +68,43 @@
     at(B + 1, op(FETCH, 0), op(NN, HID, 0, pre=1), op(NN, SKP, 1, acc=1), op(NORM, 0))
     for j in range(3):
         at(B + 2 + j, op(NN, NORMED, 2 + j, pre=2 + j), op(CAST, TRI + j))
-    at(B + 4, op(ATTEND, 0), op(ATTEND, 1))
-    at(B + 5, op(ATTEND, 2), op(ATTEND, 3), attended, op(NN, ATT, 5, pre=5), op(NORM, 1))
-    for i in range(4):
-        at(B + 6 + i, op(NN, TWO, 6 + i, pre=6 + i), op(GELU, i))
-    at(B + 9, acts, op(ROWS, 0))
+    at(B + 4, op(ATTEND, 0))
+    at(B + 5, op(ATTEND, 1), op(ATTEND, 2))
+    at(B + 6, op(ATTEND, 3), attended, op(NN, ATT, 5, pre=5), op(NORM, 1))
+    at(B + 7, op(NN, TWO, 6, pre=6), op(GELU, 0), op(NN, TWO, 7, pre=7), op(GELU, 1))
+    at(B + 8, acts, op(ROWS, 0), op(NN, TWO, 8, pre=8), op(GELU, 2), op(ROWS, 4))
+    at(B + 9, op(NN, TWO, 9, pre=9), op(GELU, 3), op(ROWS, 8), op(ROWS, 12))
     at(B + 11, op(ROWS, 1))
     at(B + 13, op(FETCH, 10), op(FETCH, 11), op(FETCH, 12))
     for i in range(4):
-        at(B + 13 + i // 2, op(NT, COT, 10 + i, post=13 + i), op(GELU_BACK, i))
-    at(B + 14, pairs)
-    at(B + 15, px, op(FULL, 0))
+        at(B + 13, op(NT, COT, 10 + i, post=13 + i), op(GELU_BACK, i))
+    at(B + 14, pairs, px, op(FULL, 0))
     for i in range(4):
-        at(B + 16 + i // 2, op(NT, EXP + 2 * i, 14 + i, acc=int(i > 0), post=17 + i))
-    at(B + 17, op(NORM_BACK, 1))
-    at(B + 18, op(NT, BR, 18, post=21), op(CAST, ATTG), op(FULL, 1))
-    at(B + 19, op(ATTEND_BACK, 0), op(ATTEND_BACK, 1))
-    at(B + 20, op(ATTEND_BACK, 2), op(ATTEND_BACK, 3), triple)
-    at(B + 21, heads, op(FULL, 2))
-    at(B + 22, op(NT, TG, 19, post=22), op(NT, TG + 2, 20, acc=1, post=23))
-    at(B + 23, op(NT, TG + 4, 21, acc=1, post=24), op(NORM_BACK, 0))
-    at(B + 24, op(FULL, 3))
-    at(B + 26, merge, op(ROWS, 2))
-    at(B + 26, sums[0], op(NT, GR, 22, post=25), op(CAST, HGRAD))
-    at(B + 27, sums[1], op(NT, GR, 23, post=26), op(CAST, SGRAD), joined)
-    at(B + 28, sums[2], op(NN, ACT, 24, post=27), op(NN, ACT + 2, 25, acc=1))
-    at(B + 29, sums[3], op(NN, ACT + 4, 26, acc=1), op(NN, ACT + 6, 27, acc=1), result)
-    at(B + 30, outs)
+        at(B + 15 + i // 2, op(NT, EXP + 2 * i, 14 + i, acc=int(i > 0), post=17 + i))
+    at(B + 16, op(NORM_BACK, 1))
+    at(B + 17, op(NT, BR, 18, post=21), op(CAST, ATTG), op(FULL, 1))
+    at(B + 18, op(ATTEND_BACK, 0), op(ATTEND_BACK, 1))
+    at(B + 19, op(ATTEND_BACK, 2), op(ATTEND_BACK, 3), triple)
+    at(B + 20, heads, op(FULL, 2))
+    at(B + 21, op(NT, TG, 19, post=22), op(NT, TG + 2, 20, acc=1, post=23))
+    at(B + 22, op(NT, TG + 4, 21, acc=1, post=24), op(NORM_BACK, 0))
+    at(B + 23, op(FULL, 3))
+    at(B + 24, merge, op(ROWS, 2))
+    at(B + 25, sums[0], op(NT, GR, 22, post=25), op(CAST, HGRAD))
+    at(B + 26, sums[1], op(NT, GR, 23, post=26), op(CAST, SGRAD), joined)
+    at(B + 27, sums[2], op(NN, ACT, 24, post=27), op(NN, ACT + 2, 25, acc=1))
+    at(B + 28, sums[3], op(NN, ACT + 4, 26, acc=1), op(NN, ACT + 6, 27, acc=1), result)
+    at(B + 29, outs)
     at(B + 32, sums[4])
-    return ops
+    spread = []
+    for tick in sorted({t for t, _ in ops}):
+        mine = [o for t, o in ops if t == tick]
+        spread += [(2 * tick + 1 + 2 * i // len(mine), o) for i, o in enumerate(mine)]
+    return spread
 
 
 OPS = plan()
-STARTS = [sum(t < tick for t, _ in OPS) for tick in range(LEAD + AHEAD + Q + 10)]
+STARTS = [sum(t < half for t, _ in OPS) for half in range(2 * (LEAD + AHEAD + Q + 10))]
 UNITS = [2, 6] + [4 * j for j in range(2, 10)] + [1 + 4 * s for s in range(4)] + [4 * j for j in (6, 7, 8, 9, 5, 2, 3, 4)] + [2, 6] + [1 + 4 * s for s in range(4)]
 
 
@@ -144,9 +148,6 @@
         ((hid.at[0], X.at[HID]), (skp.at[0], X.at[SKP]), (cot_in.at[0], X.at[COT]), (mask_in, MROWS),
          (b0, v0), (b1, v1), (b2, v2), (b3, v3), (b4, v4), (b5, v5), (b6, v6), (b7, v7)))]
     for cp in inputs: cp.start()
-    for j in range(4):
-        load_in(j).wait()
-        load_out(j, stage(j)).start()
     pl.semaphore_wait(bar, nz + 2)
 
     half = R // 2; third = half // 3
@@ -195,24 +196,33 @@
         ccopy(b, s).wait()
         xcopy(b, s).wait_send()
         ycopy(b, s).wait_send()
+    for j in range(AHEAD):
+        for d in (0, 1):
+            @pl.when(zsend_ok(d, 0))
+            def _():
+                rc(blocks[j].at[pl.ds(pl.multiple_of(base + third * zp, 16), third)], reg(z, j, base + third * zp, third),
+                   zs.at[j, d, 0], zr.at[j, d, 0], (dp, z + 1 if d == 0 else z - 1)).start()
     for j in range(4):
-        load_out(j, stage(j)).wait()
-        if j < AHEAD: own(j)
-    def gather_tick(t):
-        @pl.when(t < NB - AHEAD)
-        def _():
-            own(t + AHEAD)
-        for off, fn in ((0, zarr), (1, xarr), (2, yarr), (3, fin)):
-            for k in range(nz - 1):
-                b = t - off - k
-                @pl.when((b >= 0) & (b < NB))
-                def _():
-                    for d in (0, 1):
-                        @pl.when(zrecv_ok(d, k))
-                        def _(): fn(b, d, k)
-                        if off == 3:
-                            @pl.when(zsend_ok(d, k))
-                            def _(): zcopy(b, d, k).wait_send()
+        load_in(j).wait()
+        load_out(j, stage(j)).start()
+    for j in range(4): load_out(j, stage(j)).wait()
+    FIRST = [(zarr, 0, 0), (zarr, 0, 1), (zarr, 0, 2), (None, 0, 0)]
+    SECOND = [(xarr, 1, k) for k in range(3)] + [(yarr, 2, k) for k in range(3)] + [(fin, 3, k) for k in range(3)]
+    def gather_half(t, todo):
+        for fn, off, k in todo:
+            if fn is None:
+                @pl.when(t < NB - AHEAD)
+                def _(): own(t + AHEAD)
+                continue
+            b = t - off - k
+            @pl.when((b >= 0) & (b < NB))
+            def _():
+                for d in (0, 1):
+                    @pl.when(zrecv_ok(d, k))
+                    def _(): fn(b, d, k)
+                    if fn is fin:
+                        @pl.when(zsend_ok(d, k))
+                        def _(): zcopy(b, d, k).wait_send()
 
     T = K.shape[2]
     def ring(q): return q % RING
@@ -310,15 +320,18 @@
         cross(q).wait_send(); cross(q).wait_recv(); cross2(q).wait_send(); cross2(q).wait_recv()
     steps = [(0, start)] + [(k, functools.partial(hop, k=k)) for k in range(1, nz - 1)] + [
         (nz - 1, arrive), (nz, final), (nz + 1, relay), (nz + 3, drain)]
-    def sum_tick(t):
-        for off, fn in steps:
+    def sum_half(t, todo):
+        for off, fn in todo:
             q = t - AHEAD - off
             @pl.when((q >= 0) & (q < Q))
             def _(): fn(q)
-        @pl.when((t % SUB == 0) & (t < Q))
+    def sum_issue(t):
+        @pl.when(((t % SUB == 0) & (t > 0) & (t < Q)) | (t == 1))
         def _():
             for cp in puts(NP - 1 - t // SUB): cp.wait()
-        @pl.when(t < Q)
+        @pl.when(t == 1)
+        def _(): issue(0)
+        @pl.when((t > 0) & (t < Q))
         def _(): issue(t)
 
     devs = ((cn, z), (xn, z), (yn, z))
@@ -453,8 +466,13 @@
     def put(p):
         for cp in puts(p): cp.start()
     def pair_of(a, cols=slice(None)): return X[pl.ds(a, 2), :, cols].reshape(2 * L, -1)
-    def do_rows(kind):
+    def do_rows(a):
+        kind = a % 4
         merge = kind // 2
+        lo = a // 4
+        hi = jnp.where(kind == 0, lo + 1, 4)
+        @pl.when(kind == 0)
+        def _(): send_act(lo).wait()
         right = COT + (GR - COT) * merge
         def one(s, _):
             left = ACT + 2 * s + merge * (HID + 2 * (s // 2) - ACT - 2 * s)
@@ -464,9 +482,9 @@
                 @pl.when(cut == v)
                 def _():
                     DB[rows] = tn(pair_of(left, slice(R * v, R * v + R)), pair_of(right)).astype(bf16)
+            pltpu.make_async_copy(DB.at[rows], D.at[s, 6 - kind - 4 * merge], dsem.at[s]).start()
             return 0
-        lax.fori_loop(0, 4, one, 0)
-        put(6 - kind - 4 * merge)
+        lax.fori_loop(lo, hi, one, 0)
     def do_full(kind):
         left = jnp.where(kind < 2, TWO, jnp.where(kind == 2, NORMED + (ATT - NORMED) * c, NORMED))
         right = jnp.where(kind < 2, EXP + 2 * c + 4 * (1 - kind), jnp.where(kind == 2, TG + 4 + (BR - TG - 4) * c, TG + 2 * c))
@@ -495,7 +513,6 @@
     def x_attended(): ex["att"].start()
     def x_acts():
         arrived("cot")
-        for i in range(4): send_act(i).wait()
     def x_cot(): tally(6, X[COT].astype(f32))
     def x_pairs():
         ex["px0"].start(); ex["px1"].start()
@@ -540,14 +557,22 @@
             def _(): fn(a)
         return 0
 
-    def tick(t, _):
-        @pl.when(t < NB + nz - 2 + 3)
-        def _(): gather_tick(t)
-        @pl.when(t >= LEAD)
-        def _(): sum_tick(t - LEAD)
-        lax.fori_loop(lookup(STARTS, t), lookup(STARTS, t + 1), run, 0)
+    cut = nz - 1
+    def tick(h, _):
+        t = h // 2
+        @pl.when((h % 2 == 0) & (t < NB + nz + 2))
+        def _(): gather_half(t, FIRST)
+        @pl.when((h % 2 == 1) & (t < NB + nz + 2))
+        def _(): gather_half(t, SECOND)
+        @pl.when((h % 2 == 0) & (t >= LEAD))
+        def _(): sum_half(t - LEAD, steps[:cut])
+        @pl.when((h % 2 == 1) & (t >= LEAD))
+        def _():
+            sum_half(t - LEAD, steps[cut:])
+            sum_issue(t - LEAD)
+        lax.fori_loop(lookup(STARTS, h), lookup(STARTS, h + 1), run, 0)
         return 0
-    lax.fori_loop(0, LEAD + AHEAD + Q + nz + 3, tick, 0)
+    lax.fori_loop(0, 2 * (LEAD + AHEAD + Q + nz + 3), tick, 0)
 
 
 def block(hidden, skipped, cotangent, mask, vectors, weights, nz):
@@ -593,7 +618,11 @@
     for cp in takes[4:]: cp.start()
     for j in range(NB):
         takes[j].wait()
-        OB[j] = FB[j].astype(f32)
+        def widen(i, _):
+            part = pl.ds(pl.multiple_of(i * 32, 16), 32)
+            OB[j, part] = FB[j, part].astype(f32)
+            return 0
+        lax.fori_loop(0, R // 32, widen, 0)
         puts[j].start()
         if j == 3:
             sums.wait()

time: 325 us -> 322 us (level)
  no operation moved by 1% of the time
where the time goes in v4:
time: 322 us
  Pallas kernels  321 us (100%)
    pallas_call x1, Pallas kernels, block(): pl.pallas_call(functools.partial(block_kernel, nz=nz), out_shape=out_shap...  310 us
    pallas_call x1, Pallas kernels, unpack(): pl.pallas_call(unpack_kernel, out_shape=shapes, in_specs=[hbm] * 5, out_s...  11.5 us

profile of v4, /device:TPU:0, one launch (start us, length us, event | category | flops | bytes accessed | tf_op | source)
XLA Modules:
  0.0 321.7 jit_solution(253067747523790040)
XLA Ops:
  0.7 309.6 %shard_map.288 = (bf16[1,272,1152]{2,1,0:T(8,128)(2,1)}, bf16[1,272,1152]{2,1,0:T(8,128)(2,1)}, bf16[1,272,1152]{2,1,0:T(8,128)(2,1)}, bf16[14,288,1152]{2,1,0:T...) custom-call(bf16[1,272,1152]{2,1,0:T(8,128)(2,1)} %hid.1, ...), custom_call_target="tpu_custom_call" | custom-call | tf_op jit(solution)/shard_map/pallas_call | solution.py:599
  310.2 11.5 %shard_map.289 = (f32[576,1152]{1,0:T(8,128)}, f32[288,3456]{1,0:T(8,128)}, f32[288,1152]{1,0:T(8,128)}, f32[288,4608]{1,0:T(8,128)}, f32[1152,1152]{1,0:T(8,128...) custom-call(bf16[14,288,1152]{2,1,0:T(8,128)(2,1)} %get-tuple-elemen, ...), custom_call_target="tpu_custom_call" | custom-call | tf_op jit(solution)/shard_map/pallas_call | solution.py:648

commit v5 on v4

--- a/solution.py
+++ b/solution.py
@@ -65,20 +65,23 @@
     at(0, begin)
     at(1, stored)
     at(2, cot)
-    at(B + 1, op(FETCH, 0), op(NN, HID, 0, pre=1), op(NN, SKP, 1, acc=1), op(NORM, 0))
-    for j in range(3):
-        at(B + 2 + j, op(NN, NORMED, 2 + j, pre=2 + j), op(CAST, TRI + j))
-    at(B + 4, op(ATTEND, 0))
-    at(B + 5, op(ATTEND, 1), op(ATTEND, 2))
-    at(B + 6, op(ATTEND, 3), attended, op(NN, ATT, 5, pre=5), op(NORM, 1))
-    at(B + 7, op(NN, TWO, 6, pre=6), op(GELU, 0), op(NN, TWO, 7, pre=7), op(GELU, 1))
-    at(B + 8, acts, op(ROWS, 0), op(NN, TWO, 8, pre=8), op(GELU, 2), op(ROWS, 4))
-    at(B + 9, op(NN, TWO, 9, pre=9), op(GELU, 3), op(ROWS, 8), op(ROWS, 12))
+    halves = []
+    def by_half(tick, first, second):
+        halves.extend([(2 * tick + 1, o) for o in first] + [(2 * tick + 2, o) for o in second])
+    by_half(B + 1, [op(FETCH, 0), op(FETCH, 1)], [op(NN, HID, 0), op(NN, SKP, 1, acc=1), op(NORM, 0)])
+    by_half(B + 2, [op(FETCH, 2)], [op(NN, NORMED, 2), op(CAST, TRI)])
+    by_half(B + 3, [op(FETCH, 3)], [op(NN, NORMED, 3), op(CAST, TRI + 1)])
+    by_half(B + 4, [op(FETCH, 4)], [op(NN, NORMED, 4), op(CAST, TRI + 2), op(ATTEND, 0)])
+    by_half(B + 5, [op(FETCH, 5), op(ATTEND, 1)], [op(ATTEND, 2), op(ATTEND, 3), attended])
+    by_half(B + 6, [op(FETCH, 6), op(NN, ATT, 5), op(NORM, 1)], [op(NN, TWO, 6), op(GELU, 0)])
+    by_half(B + 7, [op(FETCH, 7), acts, op(ROWS, 0)], [op(NN, TWO, 7), op(GELU, 1)])
+    by_half(B + 8, [op(FETCH, 8), op(ROWS, 4)], [op(NN, TWO, 8), op(GELU, 2)])
+    by_half(B + 9, [op(FETCH, 9), op(ROWS, 8)], [op(NN, TWO, 9), op(GELU, 3), op(ROWS, 12)])
+    by_half(B + 13, [op(FETCH, 10), op(FETCH, 11), op(FETCH, 12)], [])
+    for i in range(4):
+        halves += [(2 * (B + 14) + i // 2, o) for o in (op(NT, COT, 10 + i, post=13 + i), op(GELU_BACK, i))]
+    halves += [(2 * (B + 14) + 1, pairs), (2 * (B + 14) + 2, px), (2 * (B + 14) + 2, op(FULL, 0))]
     at(B + 11, op(ROWS, 1))
-    at(B + 13, op(FETCH, 10), op(FETCH, 11), op(FETCH, 12))
-    for i in range(4):
-        at(B + 13, op(NT, COT, 10 + i, post=13 + i), op(GELU_BACK, i))
-    at(B + 14, pairs, px, op(FULL, 0))
     for i in range(4):
         at(B + 15 + i // 2, op(NT, EXP + 2 * i, 14 + i, acc=int(i > 0), post=17 + i))
     at(B + 16, op(NORM_BACK, 1))
@@ -100,7 +103,7 @@
     for tick in sorted({t for t, _ in ops}):
         mine = [o for t, o in ops if t == tick]
         spread += [(2 * tick + 1 + 2 * i // len(mine), o) for i, o in enumerate(mine)]
-    return spread
+    return sorted(spread + halves, key=lambda pair: pair[0])
 
 
 OPS = plan()
@@ -276,13 +279,14 @@
                 @pl.when(z == 0)
                 def _(): up(q, nz - 1 - s).start()
     def hop(q, k):
-        for s in range(nz):
+        for s in reversed(range(nz)):
             if s > k:
                 @pl.when(z == k)
                 def _():
                     got(s, q).wait_recv()
                     K[ring(q), s] = add(K[ring(q), s], R2[ring(q), s])
                     up(q, s).start()
+        for s in range(nz):
             if s < nz - 1 - k:
                 @pl.when(z == nz - 1 - k)
                 def _():

time: 322 us -> 319 us (level)
  Pallas kernels: 321 us -> 317 us
    pallas_call x1, Pallas kernels: 310 us -> 306 us  [block(): pl.pallas_call(functools.partial(block_kernel, nz=nz), out_shape=out_shap...]
where the time goes in v5:
time: 319 us; the launch traced here: 318 us
  Pallas kernels  317 us (99%)
    pallas_call x1, Pallas kernels, block(): pl.pallas_call(functools.partial(block_kernel, nz=nz), out_shape=out_shap...  306 us
    pallas_call x1, Pallas kernels, unpack(): pl.pallas_call(unpack_kernel, out_shape=shapes, in_specs=[hbm] * 5, out_s...  11.5 us

profile of v5, /device:TPU:0, one launch (start us, length us, event | category | flops | bytes accessed | tf_op | source)
XLA Modules:
  0.0 318.0 jit_solution(5088498956006340754)
XLA Ops:
  0.7 305.8 %shard_map.288 = (bf16[1,272,1152]{2,1,0:T(8,128)(2,1)}, bf16[1,272,1152]{2,1,0:T(8,128)(2,1)}, bf16[1,272,1152]{2,1,0:T(8,128)(2,1)}, bf16[14,288,1152]{2,1,0:T...) custom-call(bf16[1,272,1152]{2,1,0:T(8,128)(2,1)} %hid.1, ...), custom_call_target="tpu_custom_call" | custom-call | tf_op jit(solution)/shard_map/pallas_call | solution.py:603
  306.5 11.5 %shard_map.289 = (f32[576,1152]{1,0:T(8,128)}, f32[288,3456]{1,0:T(8,128)}, f32[288,1152]{1,0:T(8,128)}, f32[288,4608]{1,0:T(8,128)}, f32[1152,1152]{1,0:T(8,128...) custom-call(bf16[14,288,1152]{2,1,0:T(8,128)(2,1)} %get-tuple-elemen, ...), custom_call_target="tpu_custom_call" | custom-call | tf_op jit(solution)/shard_map/pallas_call | solution.py:652

commit v6 on v5

--- a/solution.py
+++ b/solution.py
@@ -76,7 +76,7 @@
     by_half(B + 6, [op(FETCH, 6), op(NN, ATT, 5), op(NORM, 1)], [op(NN, TWO, 6), op(GELU, 0)])
     by_half(B + 7, [op(FETCH, 7), acts, op(ROWS, 0)], [op(NN, TWO, 7), op(GELU, 1)])
     by_half(B + 8, [op(FETCH, 8), op(ROWS, 4)], [op(NN, TWO, 8), op(GELU, 2)])
-    by_half(B + 9, [op(FETCH, 9), op(ROWS, 8)], [op(NN, TWO, 9), op(GELU, 3), op(ROWS, 12)])
+    by_half(B + 9, [op(FETCH, 9), op(ROWS, 8), op(NN, TWO, 9), op(GELU, 3)], [op(ROWS, 12)])
     by_half(B + 13, [op(FETCH, 10), op(FETCH, 11), op(FETCH, 12)], [])
     for i in range(4):
         halves += [(2 * (B + 14) + i // 2, o) for o in (op(NT, COT, 10 + i, post=13 + i), op(GELU_BACK, i))]

time: 319 us -> 319 us (level)
  no operation moved by 1% of the time
where the time goes in v6:
time: 319 us; the launch traced here: 318 us
  Pallas kernels  317 us (99%)
    pallas_call x1, Pallas kernels, block(): pl.pallas_call(functools.partial(block_kernel, nz=nz), out_shape=out_shap...  306 us
    pallas_call x1, Pallas kernels, unpack(): pl.pallas_call(unpack_kernel, out_shape=shapes, in_specs=[hbm] * 5, out_s...  11.5 us

profile of v6, /device:TPU:0, one launch (start us, length us, event | category | flops | bytes accessed | tf_op | source)
XLA Modules:
  0.0 318.0 jit_solution(996311189656850206)
XLA Ops:
  0.7 305.8 %shard_map.288 = (bf16[1,272,1152]{2,1,0:T(8,128)(2,1)}, bf16[1,272,1152]{2,1,0:T(8,128)(2,1)}, bf16[1,272,1152]{2,1,0:T(8,128)(2,1)}, bf16[14,288,1152]{2,1,0:T...) custom-call(bf16[1,272,1152]{2,1,0:T(8,128)(2,1)} %hid.1, ...), custom_call_target="tpu_custom_call" | custom-call | tf_op jit(solution)/shard_map/pallas_call | solution.py:603
  306.5 11.5 %shard_map.289 = (f32[576,1152]{1,0:T(8,128)}, f32[288,3456]{1,0:T(8,128)}, f32[288,1152]{1,0:T(8,128)}, f32[288,4608]{1,0:T(8,128)}, f32[1152,1152]{1,0:T(8,128...) custom-call(bf16[14,288,1152]{2,1,0:T(8,128)(2,1)} %get-tuple-elemen, ...), custom_call_target="tpu_custom_call" | custom-call | tf_op jit(solution)/shard_map/pallas_call | solution.py:652
